TPU v7x, 512 devices: a whole 4x4x16 slice. The times are simulated.
512 devices in a mesh: space: 32 (over y_hi, z), rep: 16 (over y_lo, x, core).
Axes of the slice: x: 4, y: 4 (y_hi: 2, y_lo: 2; y = y_hi * 2 + y_lo), z: 16, core: 2. Of those that a mesh axis runs over, the one named last changes fastest.
Arguments:
- volumes: bfloat16 [16, 32, 8, 4, 16, 256], P('rep', 'space'), may hold values from -6 to 6
- grad_parts: bfloat16 [16, 2, 6912, 256], P('rep', None, 'space'), may hold values from -6 to 6
- master_weights: float32 [2, 6912, 256], P(None, 'space'), may hold values from -0.078125 to 0.078125
- moment_first: float32 [16, 2, 6912, 256], P('rep', None, 'space'), may hold values from -12 to 12
- moment_second: float32 [16, 2, 6912, 256], P('rep', None, 'space'), may hold values from 1 to 30
- owner: int32 [2, 32], replicated, may hold values from 0 to 15
Outputs:
- features: bfloat16 [16, 32, 8, 4, 16, 256], P('rep', 'space')
- new_weights: float32 [2, 1769472], P(None, ('space', 'rep'))
- moment_first_out: float32 [16, 2, 6912, 256], P('rep', None, 'space')
- moment_second_out: float32 [16, 2, 6912, 256], P('rep', None, 'space')
Inputs may be any that keep to these rules, and one draw needn't show every extreme that they name: owner[f, p] is the replica whose state slot holds the optimizer state of panel p of filter f, rows p * 216 to (p + 1) * 216 - 1; replicas may own unequal numbers of panels.
All inputs are finite; a program needn't handle non-finite values.
Results may differ from a plain program's by a relative error of at most 0.0095.
Values may be sent and summed in bfloat16 or wider, within the bound.
A program may use at most 64 MiB of HBM per device.

v0:
```python
import jax
import jax.numpy as jnp
from jax import lax
from jax.sharding import PartitionSpec as P

GY = 2
GZ = 2
PANEL_ROWS = 216


def passed_along(value, axis, steps):
    count = lax.axis_size(axis)
    first, last = (max(0, -steps), min(count, count - steps))
    return lax.ppermute(value, axis, [(source, source + steps) for source in range(first, last)])


def over_pieces(array, axis):
    blocks = lax.all_gather(array, axis).astype(jnp.float32)
    return blocks.sum(axis=0)


def from_root(array, axis, root):
    return lax.dynamic_index_in_dim(lax.all_gather(array, axis), root, 0, keepdims=False)


def neighbour(slab, offset):
    return passed_along(slab, "space", offset)


def keep_when(flag, slab):
    return jnp.where(flag, slab, jnp.zeros_like(slab))


def side_slab(array, dim, side):
    length = array.shape[dim]
    if side < 0:
        return lax.slice_in_dim(array, length - 1, length, 1, dim)
    return lax.slice_in_dim(array, 0, 1, 1, dim)


def extend_brick(brick, coords, strides, grid):
    lows = [coords[d] > 0 for d in range(3)]
    highs = [coords[d] < grid[d] - 1 for d in range(3)]
    current = brick
    for dim in range(3):
        lower = keep_when(lows[dim], neighbour(side_slab(current, dim, -1), strides[dim]))
        upper = keep_when(highs[dim], neighbour(side_slab(current, dim, 1), -strides[dim]))
        current = jnp.concatenate([lower, current, upper], axis=dim)
    return current


def convolve(extended, filter_rows):
    extent_x = extended.shape[0] - 2
    extent_y = extended.shape[1] - 2
    extent_z = extended.shape[2] - 2
    channels = extended.shape[3]
    summed = jnp.zeros((extent_x * extent_y * extent_z, filter_rows.shape[1]), jnp.float32)
    for shift_x in range(3):
        for shift_y in range(3):
            for shift_z in range(3):
                tap_index = (shift_x * 3 + shift_y) * 3 + shift_z
                window = extended[
                    shift_x : shift_x + extent_x,
                    shift_y : shift_y + extent_y,
                    shift_z : shift_z + extent_z,
                ]
                weights_tap = filter_rows[tap_index * channels : (tap_index + 1) * channels]
                summed = summed + jnp.dot(
                    window.reshape(-1, channels), weights_tap, preferred_element_type=jnp.float32
                )
    return summed.reshape(extent_x, extent_y, extent_z, -1)


def shards(volumes, grad_parts, master_weights, moment_first, moment_second, owner):
    filter_count = master_weights.shape[0]
    rows_dev = master_weights.shape[1]
    channels = master_weights.shape[2]
    panels_dev = rows_dev // PANEL_ROWS
    space_pos = lax.axis_index("space")
    rep_pos = lax.axis_index("rep")
    summed_grad = over_pieces(grad_parts[0].astype(jnp.float32).astype(jnp.bfloat16), "rep").astype(
        jnp.float32
    )
    first_new = 0.9 * moment_first[0] + 0.1 * summed_grad
    second_new = 0.95 * moment_second[0] + 0.05 * (summed_grad * summed_grad)
    owner_local = lax.dynamic_slice_in_dim(owner, space_pos * panels_dev, panels_dev, 1)
    owner_rows = jnp.repeat(owner_local, PANEL_ROWS, axis=1)
    owned = (owner_rows == rep_pos)[:, :, None]
    first_out = jnp.where(owned, first_new, moment_first[0])[None]
    second_out = jnp.where(owned, second_new, moment_second[0])[None]
    corr_one = 1.0 - 0.9**10
    corr_two = 1.0 - 0.95**10
    update = first_new / corr_one / (jnp.sqrt(second_new / corr_two) + 1e-08) + 0.1 * master_weights
    candidate = master_weights - 0.004 * update
    per_filter = []
    for filter_index in range(filter_count):
        slab = candidate[filter_index, 0:PANEL_ROWS]
        slabs = from_root(slab.astype(jnp.bfloat16), "rep", owner_local[filter_index, 0]).astype(
            slab.dtype
        )
        per_filter.append(slabs)
    new_master = jnp.stack(per_filter)
    share_len = rows_dev * channels // lax.axis_size("rep")
    new_weights = lax.dynamic_slice_in_dim(
        new_master.reshape(filter_count, -1), rep_pos * share_len, share_len, 1
    )
    filters = lax.all_gather(new_master.astype(jnp.bfloat16), "space", axis=1, tiled=True)
    grid = (lax.axis_size("space") // (GY * GZ), GY, GZ)
    strides = (GY * GZ, GZ, 1)
    coords = (space_pos // (GY * GZ), space_pos // GZ % GY, space_pos % GZ)
    brick = volumes[0, 0]
    hidden = jax.nn.gelu(
        convolve(extend_brick(brick, coords, strides, grid), filters[0]), approximate=True
    ).astype(jnp.bfloat16)
    output = jax.nn.gelu(
        convolve(extend_brick(hidden, coords, strides, grid), filters[1]), approximate=True
    ).astype(jnp.bfloat16)
    return (output[None, None], new_weights, first_out, second_out)


def solution(mesh):
    placed = (
        P("rep", "space", None, None, None, None),
        P("rep", None, "space", None),
        P(None, "space", None),
        P("rep", None, "space", None),
        P("rep", None, "space", None),
        P(),
    )
    return jax.shard_map(
        shards,
        mesh=mesh,
        in_specs=placed,
        out_specs=(
            P("rep", "space", None, None, None, None),
            P(None, ("space", "rep")),
            P("rep", None, "space", None),
            P("rep", None, "space", None),
        ),
        check_vma=False,
    )
```

profile of v0, /device:TPU:24, one launch (start us, length us, event | category | flops | bytes accessed | tf_op | source)
XLA Modules:
  0.0 415.0 jit_solution(16245634699472826510)
XLA Ops:
  8.0 50.1 %all-gather.5.cloned.1.call-done = bf16[16,2,216,256]{3,2,1,0:T(8,128)(2,1)} async-done(((bf16[1,2,216,256]{3,2,1,0:T(8,128)(2,1)}), bf16[16,2,216,256]{3,2,1,0:T(8,128)(2,1)}) %all-gather.5.cloned.1.call-update) | async-done | bytes 3538960 | tf_op jit(solution)/shard_map/all_gather | solution.py:18
  58.1 2.6 convert_reduce_fusion
  60.7 1.6 fusion.43
  63.8 0.9 compare_reduce_fusion
  69.1 35.6 %all-gather.9.cloned.1.call-done = bf16[16,216,256]{2,1,0:T(8,128)(2,1)} async-done(((bf16[1,216,256]{2,1,0:T(8,128)(2,1)}), bf16[16,216,256]{2,1,0:T(8,128)(2,1)}) %all-gather.9.cloned.1.call-update) | async-done | bytes 1769488 | tf_op jit(solution)/shard_map/all_gather | solution.py:23
  104.7 0.9 constant_dynamic-slice_fusion
  105.6 43.1 %all-gather.7.cloned.1.call-done = bf16[16,216,256]{2,1,0:T(8,128)(2,1)} async-done(((bf16[1,216,256]{2,1,0:T(8,128)(2,1)}), bf16[16,216,256]{2,1,0:T(8,128)(2,1)}) %all-gather.7.cloned.1.call-update) | async-done | bytes 1769488 | tf_op jit(solution)/shard_map/all_gather | solution.py:23
  148.7 0.9 constant_dynamic-slice_fusion.1
  149.6 0.7 pad_maximum_fusion.8
  150.3 7.6 %collective-permute-start = (bf16[1,4,16,256]{3,2,1,0:T(8,128)(2,1)S(1)}, bf16[1,4,16,256]{3,2,1,0:T(8,128)(2,1)S(1)}, u32[]{:S(2)}, u32[]{:S(2)}) collective-permute-start(bf16[1,4,16,256]{3,2,1,0:T(8,128)(2,1)S(1)} %get-tuple-element.78), channel_id=1, source_target_pairs={{0,64},{16,80},{32,96},{48,112},{64,128},{80,144},{96,160},{112,17... | collective-permute-start | bytes 98312 | tf_op jit(solution)/shard_map/ppermute | solution.py:14
  158.0 4.5 %collective-permute-start.1 = (bf16[1,4,16,256]{3,2,1,0:T(8,128)(2,1)S(1)}, bf16[1,4,16,256]{3,2,1,0:T(8,128)(2,1)S(1)}, u32[]{:S(2)}, u32[]{:S(2)}) collective-permute-start(bf16[1,4,16,256]{3,2,1,0:T(8,128)(2,1)S(1)} %get-tuple-element.79), channel_id=1, source_target_pairs={{64,0},{80,16},{96,32},{112,48},{128,64},{144,80},{160,96},{176,11... | collective-permute-start | bytes 98312 | tf_op jit(solution)/shard_map/ppermute | solution.py:14
  162.6 5.5 %collective-permute-done.1 = bf16[1,4,16,256]{3,2,1,0:T(8,128)(2,1)S(1)} collective-permute-done((bf16[1,4,16,256]{3,2,1,0:T(8,128)(2,1)S(1)}, bf16[1,4,16,256]{3,2,1,0:T(8,128)(2,1)S(1)}, u32[]{:S(2)}, u32[]{:S(2)}) %collective-permute-start.1) | collective-permute-done | bytes 32800 | tf_op jit(solution)/shard_map/ppermute | solution.py:14
  168.1 4.4 %collective-permute-start.2 = (bf16[10,1,16,256]{3,2,1,0:T(8,128)(2,1)S(1)}, bf16[10,1,16,256]{3,2,1,0:T(8,128)(2,1)S(1)}, u32[]{:S(2)}, u32[]{:S(2)}) collective-permute-start(bf16[10,1,16,256]{3,2,1,0:T(8,128)(2,1)S(1)} %get-tuple-element.70), channel_id=1, source_target_pairs={{0,32},{16,48},{32,64},{48,80},{64,96},{80,112},{96,128},{112,144}... | collective-permute-start | bytes 245768 | tf_op jit(solution)/shard_map/ppermute | solution.py:14
  172.5 6.0 %collective-permute-start.3 = (bf16[10,1,16,256]{3,2,1,0:T(8,128)(2,1)S(1)}, bf16[10,1,16,256]{3,2,1,0:T(8,128)(2,1)S(1)}, u32[]{:S(2)}, u32[]{:S(2)}) collective-permute-start(bf16[10,1,16,256]{3,2,1,0:T(8,128)(2,1)S(1)} %get-tuple-element.71), channel_id=1, source_target_pairs={{32,0},{48,16},{64,32},{80,48},{96,64},{112,80},{128,96},{144,112}... | collective-permute-start | bytes 245768 | tf_op jit(solution)/shard_map/ppermute | solution.py:14
  178.5 0.8 pad_maximum_fusion.6
  179.5 4.6 %collective-permute-done.3 = bf16[10,1,16,256]{3,2,1,0:T(8,128)(2,1)S(1)} collective-permute-done((bf16[10,1,16,256]{3,2,1,0:T(8,128)(2,1)S(1)}, bf16[10,1,16,256]{3,2,1,0:T(8,128)(2,1)S(1)}, u32[]{:S(2)}, u32[]{:S(2)}) %collective-permute-start.3) | collective-permute-done | bytes 81952 | tf_op jit(solution)/shard_map/ppermute | solution.py:14
  184.2 6.7 %collective-permute-start.5 = (bf16[10,6,1,256]{3,2,1,0:T(2,128)(2,1)S(1)}, bf16[10,6,1,256]{3,2,1,0:T(2,128)(2,1)S(1)}, u32[]{:S(2)}, u32[]{:S(2)}) collective-permute-start(bf16[10,6,1,256]{3,2,1,0:T(2,128)(2,1)S(1)} %get-tuple-element.48), channel_id=1, source_target_pairs={{16,0},{32,16},{48,32},{64,48},{80,64},{96,80},{112,96},{128,112},... | collective-permute-start | bytes 92168 | tf_op jit(solution)/shard_map/ppermute | solution.py:14
  190.8 1.9 collective-permute-start.4
  192.9 1.0 fusion.71
  194.0 7.2 %collective-permute-done.4 = bf16[10,6,1,256]{3,2,1,0:T(2,128)(2,1)S(1)} collective-permute-done((bf16[10,6,1,256]{3,2,1,0:T(2,128)(2,1)S(1)}, bf16[10,6,1,256]{3,2,1,0:T(2,128)(2,1)S(1)}, u32[]{:S(2)}, u32[]{:S(2)}) %collective-permute-start.4) | collective-permute-done | bytes 30752 | tf_op jit(solution)/shard_map/ppermute | solution.py:14
  201.7 1.9 fusion.67
  203.6 1.1 fusion.33
  204.7 0.9 fusion.130
  205.8 0.9 fusion.129
  206.7 0.9 copy.13
  207.6 127.3 %all-gather.11.cloned.1.call-done = bf16[2,6912,256]{2,1,0:T(8,128)(2,1)} async-done(((bf16[2,216,256]{2,1,0:T(8,128)(2,1)}), bf16[2,6912,256]{2,1,0:T(8,128)(2,1)}) %all-gather.11.cloned.1.call-update) | async-done | bytes 7077904 | tf_op jit(solution)/shard_map/all_gather | solution.py:107
  334.9 1.3 fusion.55
  336.2 1.7 fusion.52
  337.9 1.1 fusion.51
  339.0 1.2 fusion.54
  340.2 1.1 fusion.57
  341.3 1.2 fusion.58
  342.5 1.2 fusion.56
  343.7 1.1 fusion.53
  345.1 1.2 convolution_add_fusion.42
  346.6 1.2 convolution_add_fusion.40
  347.8 1.2 convolution_add_fusion.39
  352.7 4.8 %collective-permute-start.6 = (bf16[1,4,16,256]{3,2,1,0:T(8,128)(2,1)S(1)}, bf16[1,4,16,256]{3,2,1,0:T(8,128)(2,1)S(1)}, u32[]{:S(2)}, u32[]{:S(2)}) collective-permute-start(bf16[1,4,16,256]{3,2,1,0:T(8,128)(2,1)S(1)} %get-tuple-element.74), channel_id=1, source_target_pairs={{0,64},{16,80},{32,96},{48,112},{64,128},{80,144},{96,160},{112,17... | collective-permute-start | bytes 98312 | tf_op jit(solution)/shard_map/ppermute | solution.py:14
  357.6 0.7 fusion.60
  358.3 7.3 %collective-permute-start.7 = (bf16[1,4,16,256]{3,2,1,0:T(8,128)(2,1)S(1)}, bf16[1,4,16,256]{3,2,1,0:T(8,128)(2,1)S(1)}, u32[]{:S(2)}, u32[]{:S(2)}) collective-permute-start(bf16[1,4,16,256]{3,2,1,0:T(8,128)(2,1)S(1)} %get-tuple-element.75), channel_id=1, source_target_pairs={{64,0},{80,16},{96,32},{112,48},{128,64},{144,80},{160,96},{176,11... | collective-permute-start | bytes 98312 | tf_op jit(solution)/shard_map/ppermute | solution.py:14
  365.6 2.4 collective-permute-done.7
  368.0 4.0 collective-permute-start.8
  372.0 8.4 %collective-permute-start.9 = (bf16[10,1,16,256]{3,2,1,0:T(8,128)(2,1)S(1)}, bf16[10,1,16,256]{3,2,1,0:T(8,128)(2,1)S(1)}, u32[]{:S(2)}, u32[]{:S(2)}) collective-permute-start(bf16[10,1,16,256]{3,2,1,0:T(8,128)(2,1)S(1)} %get-tuple-element.67), channel_id=1, source_target_pairs={{32,0},{48,16},{64,32},{80,48},{96,64},{112,80},{128,96},{144,112}... | collective-permute-start | bytes 245768 | tf_op jit(solution)/shard_map/ppermute | solution.py:14
  380.9 1.9 collective-permute-done.9
  383.1 7.1 %collective-permute-start.11 = (bf16[10,6,1,256]{3,2,1,0:T(2,128)(2,1)S(1)}, bf16[10,6,1,256]{3,2,1,0:T(2,128)(2,1)S(1)}, u32[]{:S(2)}, u32[]{:S(2)}) collective-permute-start(bf16[10,6,1,256]{3,2,1,0:T(2,128)(2,1)S(1)} %get-tuple-element.44), channel_id=1, source_target_pairs={{16,0},{32,16},{48,32},{64,48},{80,64},{96,80},{112,96},{128,112},... | collective-permute-start | bytes 92168 | tf_op jit(solution)/shard_map/ppermute | solution.py:14
  390.2 2.1 collective-permute-start.10
  392.6 7.4 %collective-permute-done.10 = bf16[10,6,1,256]{3,2,1,0:T(2,128)(2,1)S(1)} collective-permute-done((bf16[10,6,1,256]{3,2,1,0:T(2,128)(2,1)S(1)}, bf16[10,6,1,256]{3,2,1,0:T(2,128)(2,1)S(1)}, u32[]{:S(2)}, u32[]{:S(2)}) %collective-permute-start.10) | collective-permute-done | bytes 30752 | tf_op jit(solution)/shard_map/ppermute | solution.py:14
  407.6 0.9 fusion.32
  (124 shorter events, 16.4 us)
Async XLA Ops:
  7.2 143.1 %copy-start = (bf16[1,1,8,4,16,256]{5,4,3,2,1,0:T(8,128)(2,1)S(1)}, bf16[1,1,8,4,16,256]{5,4,3,2,1,0:T(8,128)(2,1)}, u32[]{:S(2)}) copy-start(bf16[1,1,8,4,16,256]{5,4,3,2,1,0:T(8,128)(2,1)} %param.6) | copy-start | bytes 786436
  7.2 50.9 %all-gather.5.cloned.1.call-start = ((), (), s32[]{:S(2)}) async-start(), calls=%async_computation | async-start | bytes 3760128 | tf_op jit(solution)/shard_map/all_gather | solution.py:18
  7.9 96.7 %all-gather.9.cloned.1.call-start = ((), (), s32[]{:S(2)}) async-start(), calls=%async_computation.2 | async-start | bytes 1880064 | tf_op jit(solution)/shard_map/all_gather | solution.py:23
  63.0 85.6 %all-gather.7.cloned.1.call-start = ((), (), s32[]{:S(2)}) async-start(), calls=%async_computation.1 | async-start | bytes 1880064 | tf_op jit(solution)/shard_map/all_gather | solution.py:23
  63.8 271.1 %all-gather.11.cloned.1.call-start = ((), (), s32[]{:S(2)}) async-start(), calls=%async_computation.3 | async-start | bytes 7299072 | tf_op jit(solution)/shard_map/all_gather | solution.py:107
  150.3 12.3 %collective-permute-start = (bf16[1,4,16,256]{3,2,1,0:T(8,128)(2,1)S(1)}, bf16[1,4,16,256]{3,2,1,0:T(8,128)(2,1)S(1)}, u32[]{:S(2)}, u32[]{:S(2)}) collective-permute-start(bf16[1,4,16,256]{3,2,1,0:T(8,128)(2,1)S(1)} %get-tuple-element.78), channel_id=1, source_target_pairs={{0,64},{16,80},{32,96},{48,112},{64,128},{80,144},{96,160},{112,17... | collective-permute-start | bytes 98312 | tf_op jit(solution)/shard_map/ppermute | solution.py:14
  158.0 10.1 %collective-permute-start.1 = (bf16[1,4,16,256]{3,2,1,0:T(8,128)(2,1)S(1)}, bf16[1,4,16,256]{3,2,1,0:T(8,128)(2,1)S(1)}, u32[]{:S(2)}, u32[]{:S(2)}) collective-permute-start(bf16[1,4,16,256]{3,2,1,0:T(8,128)(2,1)S(1)} %get-tuple-element.79), channel_id=1, source_target_pairs={{64,0},{80,16},{96,32},{112,48},{128,64},{144,80},{160,96},{176,11... | collective-permute-start | bytes 98312 | tf_op jit(solution)/shard_map/ppermute | solution.py:14
  168.1 11.3 %collective-permute-start.2 = (bf16[10,1,16,256]{3,2,1,0:T(8,128)(2,1)S(1)}, bf16[10,1,16,256]{3,2,1,0:T(8,128)(2,1)S(1)}, u32[]{:S(2)}, u32[]{:S(2)}) collective-permute-start(bf16[10,1,16,256]{3,2,1,0:T(8,128)(2,1)S(1)} %get-tuple-element.70), channel_id=1, source_target_pairs={{0,32},{16,48},{32,64},{48,80},{64,96},{80,112},{96,128},{112,144}... | collective-permute-start | bytes 245768 | tf_op jit(solution)/shard_map/ppermute | solution.py:14
  172.5 11.6 %collective-permute-start.3 = (bf16[10,1,16,256]{3,2,1,0:T(8,128)(2,1)S(1)}, bf16[10,1,16,256]{3,2,1,0:T(8,128)(2,1)S(1)}, u32[]{:S(2)}, u32[]{:S(2)}) collective-permute-start(bf16[10,1,16,256]{3,2,1,0:T(8,128)(2,1)S(1)} %get-tuple-element.71), channel_id=1, source_target_pairs={{32,0},{48,16},{64,32},{80,48},{96,64},{112,80},{128,96},{144,112}... | collective-permute-start | bytes 245768 | tf_op jit(solution)/shard_map/ppermute | solution.py:14
  184.2 9.7 %collective-permute-start.5 = (bf16[10,6,1,256]{3,2,1,0:T(2,128)(2,1)S(1)}, bf16[10,6,1,256]{3,2,1,0:T(2,128)(2,1)S(1)}, u32[]{:S(2)}, u32[]{:S(2)}) collective-permute-start(bf16[10,6,1,256]{3,2,1,0:T(2,128)(2,1)S(1)} %get-tuple-element.48), channel_id=1, source_target_pairs={{16,0},{32,16},{48,32},{64,48},{80,64},{96,80},{112,96},{128,112},... | collective-permute-start | bytes 92168 | tf_op jit(solution)/shard_map/ppermute | solution.py:14
  190.8 10.3 %collective-permute-start.4 = (bf16[10,6,1,256]{3,2,1,0:T(2,128)(2,1)S(1)}, bf16[10,6,1,256]{3,2,1,0:T(2,128)(2,1)S(1)}, u32[]{:S(2)}, u32[]{:S(2)}) collective-permute-start(bf16[10,6,1,256]{3,2,1,0:T(2,128)(2,1)S(1)} %get-tuple-element.49), channel_id=1, source_target_pairs={{0,16},{16,32},{32,48},{48,64},{64,80},{80,96},{96,112},{112,128},... | collective-permute-start | bytes 92168 | tf_op jit(solution)/shard_map/ppermute | solution.py:14
  192.9 10.7 %copy-start.2 = (f32[1,2,216,256]{3,2,1,0:T(8,128)S(1)}, f32[1,2,216,256]{3,2,1,0:T(8,128)}, u32[]{:S(2)}) copy-start(f32[1,2,216,256]{3,2,1,0:T(8,128)} %param.10) | copy-start | bytes 1327108
  192.9 10.7 %copy-start.3 = (f32[1,2,216,256]{3,2,1,0:T(8,128)S(1)}, f32[1,2,216,256]{3,2,1,0:T(8,128)}, u32[]{:S(2)}) copy-start(f32[1,2,216,256]{3,2,1,0:T(8,128)} %param.9) | copy-start | bytes 1327108
  207.6 141.4 %copy-start.14 = (bf16[8,4,16,256]{3,2,1,0:T(8,128)(2,1)S(1)}, bf16[8,4,16,256]{3,2,1,0:T(8,128)(2,1)}, u32[]{:S(2)}) copy-start(bf16[8,4,16,256]{3,2,1,0:T(8,128)(2,1)} %get-tuple-element.31) | copy-start | bytes 786436
  334.9 10.0 %copy-start.1 = (bf16[2,6912,256]{2,1,0:T(8,128)(2,1)S(1)}, bf16[2,6912,256]{2,1,0:T(8,128)(2,1)}, u32[]{:S(2)}) copy-start(bf16[2,6912,256]{2,1,0:T(8,128)(2,1)} %all-gather.11.cloned.1.call-done) | copy-start | bytes 21233668
  334.9 11.4 %copy-start.15 = (bf16[8,4,16,256]{3,2,1,0:T(8,128)(2,1)S(1)}, bf16[8,4,16,256]{3,2,1,0:T(8,128)(2,1)}, u32[]{:S(2)}) copy-start(bf16[8,4,16,256]{3,2,1,0:T(8,128)(2,1)} %get-tuple-element.32) | copy-start | bytes 786436
  336.2 13.0 %copy-start.13 = (bf16[8,4,16,256]{3,2,1,0:T(8,128)(2,1)S(1)}, bf16[8,4,16,256]{3,2,1,0:T(8,128)(2,1)}, u32[]{:S(2)}) copy-start(bf16[8,4,16,256]{3,2,1,0:T(8,128)(2,1)} %get-tuple-element.86) | copy-start | bytes 786436
  339.0 10.4 %copy-start.5 = (bf16[8,4,16,256]{3,2,1,0:T(8,128)(2,1)S(1)}, bf16[8,4,16,256]{3,2,1,0:T(8,128)(2,1)}, u32[]{:S(2)}) copy-start(bf16[8,4,16,256]{3,2,1,0:T(8,128)(2,1)} %get-tuple-element.60) | copy-start | bytes 786436
  341.3 8.4 %copy-start.12 = (bf16[8,4,16,256]{3,2,1,0:T(8,128)(2,1)S(1)}, bf16[8,4,16,256]{3,2,1,0:T(8,128)(2,1)}, u32[]{:S(2)}) copy-start(bf16[8,4,16,256]{3,2,1,0:T(8,128)(2,1)} %get-tuple-element.30) | copy-start | bytes 786436
  342.5 7.4 %copy-start.11 = (bf16[8,4,16,256]{3,2,1,0:T(8,128)(2,1)S(1)}, bf16[8,4,16,256]{3,2,1,0:T(8,128)(2,1)}, u32[]{:S(2)}) copy-start(bf16[8,4,16,256]{3,2,1,0:T(8,128)(2,1)} %get-tuple-element.87) | copy-start | bytes 786436
  344.8 5.4 %copy-start.4 = (bf16[8,4,16,256]{3,2,1,0:T(8,128)(2,1)S(1)}, bf16[8,4,16,256]{3,2,1,0:T(8,128)(2,1)}, u32[]{:S(2)}) copy-start(bf16[8,4,16,256]{3,2,1,0:T(8,128)(2,1)} %get-tuple-element.95) | copy-start | bytes 786436
  345.1 5.3 %copy-start.10 = (bf16[8,4,16,256]{3,2,1,0:T(8,128)(2,1)S(1)}, bf16[8,4,16,256]{3,2,1,0:T(8,128)(2,1)}, u32[]{:S(2)}) copy-start(bf16[8,4,16,256]{3,2,1,0:T(8,128)(2,1)} %get-tuple-element.29) | copy-start | bytes 786436
  346.3 4.4 %copy-start.9 = (bf16[8,4,16,256]{3,2,1,0:T(8,128)(2,1)S(1)}, bf16[8,4,16,256]{3,2,1,0:T(8,128)(2,1)}, u32[]{:S(2)}) copy-start(bf16[8,4,16,256]{3,2,1,0:T(8,128)(2,1)} %get-tuple-element.88) | copy-start | bytes 786436
  349.4 1.9 copy-start.16
  349.7 1.9 copy-start.8
  349.9 1.9 copy-start.7
  350.4 1.8 copy-start.6
  350.9 6.6 %copy-start.17 = (bf16[1,1,216,256]{3,1,2,0:T(2,128)(2,1)S(1)}, bf16[1,1,216,256]{3,1,2,0:T(2,128)(2,1)}, u32[]{:S(2)}) copy-start(bf16[1,1,216,256]{3,1,2,0:T(2,128)(2,1)} %copy.13) | copy-start | bytes 331780
  352.7 12.9 %collective-permute-start.6 = (bf16[1,4,16,256]{3,2,1,0:T(8,128)(2,1)S(1)}, bf16[1,4,16,256]{3,2,1,0:T(8,128)(2,1)S(1)}, u32[]{:S(2)}, u32[]{:S(2)}) collective-permute-start(bf16[1,4,16,256]{3,2,1,0:T(8,128)(2,1)S(1)} %get-tuple-element.74), channel_id=1, source_target_pairs={{0,64},{16,80},{32,96},{48,112},{64,128},{80,144},{96,160},{112,17... | collective-permute-start | bytes 98312 | tf_op jit(solution)/shard_map/ppermute | solution.py:14
  358.3 9.7 %collective-permute-start.7 = (bf16[1,4,16,256]{3,2,1,0:T(8,128)(2,1)S(1)}, bf16[1,4,16,256]{3,2,1,0:T(8,128)(2,1)S(1)}, u32[]{:S(2)}, u32[]{:S(2)}) collective-permute-start(bf16[1,4,16,256]{3,2,1,0:T(8,128)(2,1)S(1)} %get-tuple-element.75), channel_id=1, source_target_pairs={{64,0},{80,16},{96,32},{112,48},{128,64},{144,80},{160,96},{176,11... | collective-permute-start | bytes 98312 | tf_op jit(solution)/shard_map/ppermute | solution.py:14
  368.0 12.9 %collective-permute-start.8 = (bf16[10,1,16,256]{3,2,1,0:T(8,128)(2,1)S(1)}, bf16[10,1,16,256]{3,2,1,0:T(8,128)(2,1)S(1)}, u32[]{:S(2)}, u32[]{:S(2)}) collective-permute-start(bf16[10,1,16,256]{3,2,1,0:T(8,128)(2,1)S(1)} %get-tuple-element.66), channel_id=1, source_target_pairs={{0,32},{16,48},{32,64},{48,80},{64,96},{80,112},{96,128},{112,144}... | collective-permute-start | bytes 245768 | tf_op jit(solution)/shard_map/ppermute | solution.py:14
  372.0 10.8 %collective-permute-start.9 = (bf16[10,1,16,256]{3,2,1,0:T(8,128)(2,1)S(1)}, bf16[10,1,16,256]{3,2,1,0:T(8,128)(2,1)S(1)}, u32[]{:S(2)}, u32[]{:S(2)}) collective-permute-start(bf16[10,1,16,256]{3,2,1,0:T(8,128)(2,1)S(1)} %get-tuple-element.67), channel_id=1, source_target_pairs={{32,0},{48,16},{64,32},{80,48},{96,64},{112,80},{128,96},{144,112}... | collective-permute-start | bytes 245768 | tf_op jit(solution)/shard_map/ppermute | solution.py:14
  383.1 9.4 %collective-permute-start.11 = (bf16[10,6,1,256]{3,2,1,0:T(2,128)(2,1)S(1)}, bf16[10,6,1,256]{3,2,1,0:T(2,128)(2,1)S(1)}, u32[]{:S(2)}, u32[]{:S(2)}) collective-permute-start(bf16[10,6,1,256]{3,2,1,0:T(2,128)(2,1)S(1)} %get-tuple-element.44), channel_id=1, source_target_pairs={{16,0},{32,16},{48,32},{64,48},{80,64},{96,80},{112,96},{128,112},... | collective-permute-start | bytes 92168 | tf_op jit(solution)/shard_map/ppermute | solution.py:14
  390.2 9.7 %collective-permute-start.10 = (bf16[10,6,1,256]{3,2,1,0:T(2,128)(2,1)S(1)}, bf16[10,6,1,256]{3,2,1,0:T(2,128)(2,1)S(1)}, u32[]{:S(2)}, u32[]{:S(2)}) collective-permute-start(bf16[10,6,1,256]{3,2,1,0:T(2,128)(2,1)S(1)} %get-tuple-element.45), channel_id=1, source_target_pairs={{0,16},{16,32},{32,48},{48,64},{64,80},{80,96},{96,112},{112,128},... | collective-permute-start | bytes 92168 | tf_op jit(solution)/shard_map/ppermute | solution.py:14
Sparse Core Ops, SparseCore 0:
  10.1 47.9 all-gather.4
  63.2 41.4 all-gather.8
  107.4 41.2 all-gather.6
  151.6 183.2 all-gather.10
where the time goes:
time: 416 us; the launch traced here: 415 us
  waiting for transfers between devices  287 us (69%)
  starting transfers between devices  65 us (16%)
  matrix products  23.4 us (6%)
  between operations  18.6 us (4%)
  other arithmetic  11.2 us (3%)
  local copies, waits for them, and re-layouts  9.75 us (2%)
    all_gather x1, waiting for transfers between devices, shards(): lax.all_gather(new_master.astype(jnp.bfloat16), 'space', axis=1, tiled=True)  127 us
    all_gather x2, waiting for transfers between devices, from_root(): lax.all_gather(array, axis)  78.7 us
    ppermute x12, starting transfers between devices, passed_along(): lax.ppermute(value, axis, [(source, source + steps) for source in range(f...  64.9 us
    all_gather x1, waiting for transfers between devices, over_pieces(): blocks = lax.all_gather(array, axis).astype(jnp.float32)  50.1 us
    ppermute x12, waiting for transfers between devices, passed_along(): lax.ppermute(value, axis, [(source, source + steps) for source in range(f...  29.5 us
    dot_general x54, matrix products, convolve(): jnp.dot(window.reshape(-1, channels), weights_tap, preferred_element_type...  23.4 us
  transfers between devices with their start and end apart: 16, of which 12 were waited for; matrix products, arithmetic and copies ran while one was open for 3% of the time, Pallas kernels for 0%

commit v1 on v0

v1 whole, which is shorter than its diff:
```python
import jax
import jax.numpy as jnp
from jax import lax
from jax.experimental import pallas as pl
from jax.experimental.pallas import tpu as pltpu
from jax.sharding import PartitionSpec as P

MESH = pl.DeviceIdType.MESH
F32 = jnp.float32
BF16 = jnp.bfloat16
UNITS = 27
ZS = 16
N_A2A, N_HALO, N_Z, N_RING, N_SIB, N_G = 15, 6, 15, 32, 16, 15


def unit_of(row_unit):
    panel, within = divmod(row_unit, UNITS)
    group, place = divmod(within, 7)
    return panel // ZS, panel % ZS, group // 2, group % 2, place


def runs_of(chunk):
    runs = []
    for k in range(96):
        at = unit_of(96 * chunk + k)
        if runs and runs[-1][1][:4] == at[:4] and runs[-1][1][4] + runs[-1][2] == at[4]:
            runs[-1][2] += 1
        else:
            runs.append([k, at, 1])
    return runs


def gelu(v):
    return 0.5 * v * (1.0 + jnp.tanh(0.7978845608028654 * (v + 0.044715 * (v * v * v))))


def body(
    owner, vol, grads, master, mom1, mom2,
    feat, pan, mom1_out, mom2_out,
    stage, got, gsum, gall, filt, raw, edge_out, edge_in, field, acc, hid, wbuf,
    bar_send, bar_recv,
):
    s = lax.axis_index("space")
    r = lax.axis_index("rep")
    yhi, z = s // ZS, lax.rem(s, ZS)
    ylo, x, c = r // 8, lax.rem(r // 2, 4), lax.rem(r, 2)
    y = 2 * yhi + ylo
    bx, by, bz = s // 4, lax.rem(s // 2, 2), lax.rem(s, 2)

    def device(px, py, pz, pc):
        return (py // 2 * ZS + pz, lax.rem(py, 2) * 8 + 2 * px + pc)

    xp, xm = lax.rem(x + 1, 4), lax.rem(x + 3, 4)
    yp, ym = lax.rem(y + 1, 4), lax.rem(y + 3, 4)
    zp, zm = lax.rem(z + 1, ZS), lax.rem(z + ZS - 1, ZS)
    other_y = jnp.where(ylo == 0, ym, yp)
    peers = [(s, lax.rem(r + d, 16)) for d in range(1, 16)]
    z_peers = [device(x, y, zp, c), device(x, y, zm, c), device(x, other_y, z, c)]
    flip = 2 - 4 * by
    halo_peers = []
    for dx, fl in ((-1, 0), (1, 0), (0, 1), (-1, 1), (1, 1)):
        halo_peers.append((dx, fl, (lax.rem(s + fl * flip + 4 * dx + 32, 32), r)))

    barrier = pltpu.get_barrier_semaphore()
    all_peers = peers + z_peers + [p for _, _, p in halo_peers]
    for p in all_peers:
        pl.semaphore_signal(barrier, inc=1, device_id=p, device_id_type=MESH)

    for d in range(16):
        dl, dx, dc = d // 8, d // 2 % 4, d % 2
        first = 7 * (2 * dc + dl) + 2 * dx
        for u in range(2):
            at = min(first + (u if dx < 3 else 0), UNITS - 1)
            stage[d, :, 0, u] = grads[:, at]
            stage[d, :, 1, u] = mom1[:, at].astype(BF16)
            stage[d, :, 2, u] = mom2[:, at].astype(BF16)

    pl.semaphore_wait(barrier, len(all_peers))

    sent = []
    base = [0]

    def take(n):
        base[0] += n
        return base[0] - n

    def send(src, dst, k, dev):
        copy = pltpu.make_async_remote_copy(
            src_ref=src, dst_ref=dst, send_sem=bar_send.at[k], recv_sem=bar_recv.at[k],
            device_id=dev, device_id_type=MESH,
        )
        copy.start()
        sent.append(copy)

    def arrived(dst, k):
        pltpu.make_async_remote_copy(
            src_ref=dst, dst_ref=dst, send_sem=bar_send.at[k], recv_sem=bar_recv.at[k],
            device_id=(s, r), device_id_type=MESH,
        ).wait_recv()

    a2a = take(N_A2A)
    for d in range(1, 16):
        to = lax.rem(r + d, 16)
        send(stage.at[to], got.at[r], a2a + d - 1, (s, to))
    halo = take(N_HALO)
    x_src = {-1: (0, 2), 0: (0, 8), 1: (6, 2)}
    x_dst = {-1: 10, 0: 2, 1: 0}
    for k, (dx, fl, dev) in enumerate(halo_peers):
        sx, nx = x_src[dx]
        sy, dy, ny = (2 * (1 - by), 6 * by, 2) if fl else (0, 2, 4)
        send(
            vol.at[pl.ds(sx, nx), pl.ds(sy, ny)],
            raw.at[pl.ds(x_dst[dx], nx), pl.ds(dy, ny)],
            halo + k, dev,
        )
    got[r] = stage[r]
    raw[2:10, 2:6] = vol[...]

    for d in range(1, 16):
        arrived(got.at[lax.rem(r + 16 - d, 16)], a2a + d - 1)
    first = 7 * (2 * c + ylo) + 2 * x
    corr_one = 1.0 - 0.9**10
    corr_two = 1.0 - 0.95**10
    for f in range(2):
        own = owner[f, s]
        for u in range(2):
            total = got[0, f, 0, u].astype(F32)
            for k in range(1, 16):
                total = total + got[k, f, 0, u].astype(F32)
            m_new = 0.9 * got[own, f, 1, u].astype(F32) + 0.1 * total
            v_new = 0.95 * got[own, f, 2, u].astype(F32) + 0.05 * (total * total)
            w = master[f, jnp.minimum(first + u, UNITS - 1)]
            step = m_new / corr_one / (jnp.sqrt(v_new / corr_two) + 1e-08) + 0.1 * w
            gsum[f, u] = total.astype(BF16)
            filt[f, yhi, z, c, ylo, 2 * x + u] = (w - 0.004 * step).astype(BF16)

    zb = take(N_Z)

    def z_block(pz):
        return filt.at[:, yhi, pz, c, ylo, pl.ds(2 * x, 2)]

    for k in range(8):
        up, down = lax.rem(z + ZS - k, ZS), lax.rem(z + k, ZS)
        if k:
            arrived(z_block(up), zb + 2 * (k - 1))
        send(z_block(up), z_block(up), zb + 2 * k, device(x, y, zp, c))
        if k:
            arrived(z_block(down), zb + 2 * (k - 1) + 1)
        if k < 7:
            send(z_block(down), z_block(down), zb + 2 * k + 1, device(x, y, zm, c))
    arrived(z_block(lax.rem(z + 8, ZS)), zb + 14)

    ring = take(N_RING)
    sib = take(N_SIB)
    sib_dev = device(x, y, z, 1 - c)

    def region(f, half, phase, pos, part, core):
        z0, nz = 8 * half + (4 if part == 1 else 0), 8 if part is None else 4
        zr = pl.ds(z0, nz)
        if half == 0 and phase == 0:
            return filt.at[f, yhi, zr, core, ylo, pl.ds(2 * pos, 2)]
        if half == 0:
            return filt.at[f, pos // 2, zr, core, lax.rem(pos, 2), pl.ds(0, 7)]
        if phase == 0:
            return filt.at[f, pos // 2, zr, core, lax.rem(pos, 2), pl.ds(2 * x, 2)]
        return filt.at[f, :, zr, core, :, pl.ds(2 * pos, 2)]

    def ring_of(f, half, phase):
        k = ring + 4 * (4 * f + 2 * half + phase)
        if half == phase:
            me, plus, minus, opp = x, xp, xm, lax.rem(x + 2, 4)
            to_plus, to_minus = device(xp, y, z, c), device(xm, y, z, c)
        else:
            me, plus, minus, opp = y, yp, ym, lax.rem(y + 2, 4)
            to_plus, to_minus = device(x, yp, z, c), device(x, ym, z, c)

        def reg(pos, part=None, core=c):
            return region(f, half, phase, pos, part, core)

        return k, me, plus, minus, opp, to_plus, to_minus, reg

    def start_one(f, half, phase):
        k, me, plus, minus, opp, to_plus, to_minus, reg = ring_of(f, half, phase)
        send(reg(me), reg(me), k, to_plus)
        send(reg(me), reg(me), k + 1, to_minus)

    def turn(f, half, phase):
        k, me, plus, minus, opp, to_plus, to_minus, reg = ring_of(f, half, phase)
        arrived(reg(minus), k)
        send(reg(minus, 0), reg(minus, 0), k + 2, to_plus)
        arrived(reg(plus), k + 1)
        send(reg(plus, 1), reg(plus, 1), k + 3, to_minus)
        if phase == 1:
            q = sib + 8 * f + 4 * half + 1
            send(reg(minus), reg(minus), q, sib_dev)
            send(reg(plus), reg(plus), q + 1, sib_dev)

    def end(f, half, phase):
        k, me, plus, minus, opp, to_plus, to_minus, reg = ring_of(f, half, phase)
        arrived(reg(opp, 0), k + 2)
        arrived(reg(opp, 1), k + 3)
        if phase == 1:
            q = sib + 8 * f + 4 * half + 3
            send(reg(opp), reg(opp), q, sib_dev)

    def bulk(f, half):
        k, me, plus, minus, opp, to_plus, to_minus, reg = ring_of(f, half, 1)
        start_one(f, half, 1)
        send(reg(me), reg(me), sib + 8 * f + 4 * half, sib_dev)

    def from_sib(f):
        for half in range(2):
            k, me, plus, minus, opp, to_plus, to_minus, reg = ring_of(f, half, 1)
            for n, pos in enumerate((me, minus, plus, opp)):
                arrived(reg(pos, None, 1 - c), sib + 8 * f + 4 * half + n)

    for f in range(2):
        start_one(f, 0, 0)
        start_one(f, 1, 0)
    for f in range(2):
        turn(f, 0, 0)
        turn(f, 1, 0)
        end(f, 0, 0)
        bulk(f, 0)
        end(f, 1, 0)
        bulk(f, 1)

    for k, (dx, fl, dev) in enumerate(halo_peers):
        sx, nx = x_src[dx]
        dy, ny = (6 * (1 - by), 2) if fl else (2, 4)
        dst_x = {-1: 0, 0: 2, 1: 10}[dx]
        pairs = raw.at[pl.ds(dst_x, nx), pl.ds(dy, ny)]
        arrived(pairs, halo + {0: 1, 1: 0, 2: 2, 3: 4, 4: 3}[k])

    def pack(i, carry):
        rows = [raw[i, j].astype(F32) for j in range(8)]
        near = jnp.concatenate([jnp.where(bz == 0, v[15:16], v[0:1]) for v in rows], axis=0)
        far = jnp.concatenate([jnp.where(bz == 0, v[14:15], v[1:2]) for v in rows], axis=0)
        edge_out[i] = jnp.concatenate([near, far], axis=0).astype(BF16)
        return carry

    lax.fori_loop(0, 12, pack, 0)
    z_partner = z + 1 - 2 * bz
    send(edge_out, edge_in, halo + 5, device(x, y, z_partner, c))
    arrived(edge_in, halo + 5)

    def shifts(i, carry):
        edges = edge_in[i].astype(F32)
        x_ok = (i + 8 * bx >= 2) & (i + 8 * bx < 66)
        for j in range(8):
            y_ok = (j + 4 * by >= 2) & (j + 4 * by < 10)
            ok = x_ok & y_ok
            v = jnp.where(ok, raw[i, j].astype(F32), 0.0)
            e0 = jnp.where(ok, edges[j : j + 1], 0.0)
            e1 = jnp.where(ok, edges[8 + j : 9 + j], 0.0)
            none = jnp.zeros((1, 256), F32)
            rest = jnp.zeros((7, 256), F32)
            low = bz == 0
            field[i, j, :, 0:256] = jnp.concatenate(
                [jnp.where(low, none, e0), v[0:15], jnp.where(low, v[15:16], e1), rest], axis=0
            ).astype(BF16)
            field[i, j, :, 256:512] = jnp.concatenate([v, e0, rest], axis=0).astype(BF16)
            field[i, j, :, 512:768] = jnp.concatenate(
                [v[1:16], jnp.where(low, e0, none), jnp.where(low, e1, v[0:1]), rest], axis=0
            ).astype(BF16)
        return carry

    lax.fori_loop(0, 12, shifts, 0)

    for f in range(2):
        for half in range(2):
            turn(f, half, 1)
        for half in range(2):
            end(f, half, 1)

    gs = take(N_G)
    for d in range(1, 16):
        to = lax.rem(r + d, 16)
        send(gsum, gall.at[r], gs + d - 1, (s, to))
    gall[r] = gsum[...]

    def load_chunk(f, n):
        for k, (a, b, cc, d, u), count in runs_of(n):
            wbuf[k : k + count] = filt[f, a, b, cc, d, u : u + count]

    from_sib(0)
    y_at = 1 - by
    for n in range(9):
        a, b = divmod(n, 3)
        load_chunk(0, n)

        def one(i, carry, a=a, b=b, n=n):
            lhs = field[pl.ds(2 * i + a, 2), pl.ds(y_at + b, 5)].reshape(240, 768)
            part = jnp.dot(lhs, wbuf[...].reshape(768, 256), preferred_element_type=F32)
            rows = pl.ds(2 * i, 2)
            part = part.reshape(2, 5, 24, 256)
            acc[rows] = part if n == 0 else acc[rows] + part
            return carry

        lax.fori_loop(0, 5, one, 0)

    def activate(i, carry):
        ok = (i + 8 * bx >= 1) & (i + 8 * bx < 65)
        low = bz == 0
        hid[i, 5 * by] = jnp.zeros((16, 768), BF16)
        for j in range(5):
            h = jnp.where(ok, gelu(acc[i, j]), 0.0)
            none = jnp.zeros((1, 256), F32)
            edge = h[16:17]
            hid[i, y_at + j, :, 0:256] = jnp.concatenate(
                [jnp.where(low, none, edge), h[0:15]], axis=0
            ).astype(BF16)
            hid[i, y_at + j, :, 256:512] = h[0:16].astype(BF16)
            hid[i, y_at + j, :, 512:768] = jnp.concatenate(
                [h[1:16], jnp.where(low, edge, none)], axis=0
            ).astype(BF16)
        return carry

    lax.fori_loop(0, 10, activate, 0)

    from_sib(1)
    for n in range(9):
        a, b = divmod(n, 3)
        load_chunk(1, n)

        def two(i, carry, a=a, b=b, n=n):
            lhs = hid[pl.ds(4 * i + a, 4), b : b + 4].reshape(256, 768)
            part = jnp.dot(lhs, wbuf[...].reshape(768, 256), preferred_element_type=F32)
            rows = pl.ds(4 * i, 4)
            part = part.reshape(4, 4, 16, 256)
            acc[rows, 0:4, 0:16] = part if n == 0 else acc[rows, 0:4, 0:16] + part
            return carry

        lax.fori_loop(0, 2, two, 0)

    def finish(i, carry):
        feat[i] = gelu(acc[i, 0:4, 0:16]).astype(BF16)
        return carry

    lax.fori_loop(0, 8, finish, 0)

    for d in range(1, 16):
        arrived(gall.at[lax.rem(r + 16 - d, 16)], gs + d - 1)
    for f in range(2):
        owned = owner[f, s] == r
        for d in range(16):
            dl, dx, dc = d // 8, d // 2 % 4, d % 2
            for u in range(2):
                at = 7 * (2 * dc + dl) + 2 * dx + u
                if 2 * dx + u > 6 or at >= UNITS:
                    continue
                g = gall[d, f, u].astype(F32)
                m, v = mom1[f, at], mom2[f, at]
                mom1_out[f, at] = jnp.where(owned, 0.9 * m + 0.1 * g, m)
                mom2_out[f, at] = jnp.where(owned, 0.95 * v + 0.05 * (g * g), v)
                pan[f, at] = filt[f, yhi, z, dc, dl, 2 * dx + u]
    for copy in sent:
        copy.wait_send()


def shards(volumes, grad_parts, master, mom1, mom2, owner):
    def units(a):
        return a.reshape(2, UNITS, 8, 256)

    vmem = pl.BlockSpec(memory_space=pltpu.VMEM)
    n_sems = N_A2A + N_HALO + N_Z + N_RING + N_SIB + N_G
    state = jax.ShapeDtypeStruct((2, UNITS, 8, 256), F32)
    feat, pan, m_out, v_out = pl.pallas_call(
        body,
        out_shape=(
            jax.ShapeDtypeStruct((8, 4, 16, 256), BF16),
            jax.ShapeDtypeStruct((2, UNITS, 8, 256), BF16),
            state,
            state,
        ),
        in_specs=[pl.BlockSpec(memory_space=pltpu.SMEM)] + [vmem] * 5,
        out_specs=[vmem] * 4,
        scratch_shapes=[
            pltpu.VMEM((16, 2, 3, 2, 8, 256), BF16),
            pltpu.VMEM((16, 2, 3, 2, 8, 256), BF16),
            pltpu.VMEM((2, 2, 8, 256), BF16),
            pltpu.VMEM((16, 2, 2, 8, 256), BF16),
            pltpu.VMEM((2, 2, ZS, 2, 2, 8, 8, 256), BF16),
            pltpu.VMEM((12, 8, 16, 256), BF16),
            pltpu.VMEM((12, 16, 256), BF16),
            pltpu.VMEM((12, 16, 256), BF16),
            pltpu.VMEM((12, 8, 24, 768), BF16),
            pltpu.VMEM((10, 5, 24, 256), F32),
            pltpu.VMEM((10, 6, 16, 768), BF16),
            pltpu.VMEM((96, 8, 256), BF16),
            pltpu.SemaphoreType.DMA((n_sems,)),
            pltpu.SemaphoreType.DMA((n_sems,)),
        ],
        compiler_params=pltpu.CompilerParams(
            collective_id=0, has_side_effects=True, vmem_limit_bytes=56 << 20
        ),
    )(owner, volumes[0, 0], units(grad_parts[0]), units(master), units(mom1[0]), units(mom2[0]))
    share = lax.dynamic_slice_in_dim(
        pan.reshape(2, UNITS * 2048), lax.axis_index("rep") * 3456, 3456, 1
    ).astype(F32)
    return (
        feat[None, None],
        share,
        m_out.reshape(1, 2, 216, 256),
        v_out.reshape(1, 2, 216, 256),
    )


def solution(mesh):
    placed = (
        P("rep", "space", None, None, None, None),
        P("rep", None, "space", None),
        P(None, "space", None),
        P("rep", None, "space", None),
        P("rep", None, "space", None),
        P(),
    )
    return jax.shard_map(
        shards,
        mesh=mesh,
        in_specs=placed,
        out_specs=(
            P("rep", "space", None, None, None, None),
            P(None, ("space", "rep")),
            P("rep", None, "space", None),
            P("rep", None, "space", None),
        ),
        check_vma=False,
    )
```

time: 416 us -> 109 us (0.26)
  the two profiles are of different devices: /device:TPU:24 before, /device:TPU:1 now
where the time goes in v1:
time: 109 us; the launch traced here: 108 us
  Pallas kernels  103 us (94%)
  local copies, waits for them, and re-layouts  3.82 us (4%)
    pallas_call x1, Pallas kernels, shards(): pl.pallas_call(body, out_shape=(jax.ShapeDtypeStruct((8, 4, 16, 256), BF1...  103 us
    unnamed x10, local copies, waits for them, and re-layouts  3.82 us

profile of v1, /device:TPU:1, one launch (start us, length us, event | category | flops | bytes accessed | tf_op | source)
XLA Modules:
  0.0 107.7 jit_solution(2190351693688407679)
XLA Ops:
  0.6 102.5 %shard_map.93 = (bf16[8,4,16,256]{3,2,1,0:T(8,128)(2,1)}, bf16[2,27,8,256]{3,2,1,0:T(8,128)(2,1)}, f32[2,27,8,256]{3,2,1,0:T(8,128)}, f32[2,27,8,256]{3,2,1,0:T(8,128)}) custom-call(s32[2,32]{1,0:T(2,128)} %owner.1, bf16[8,4,16,256]{3,2,1,0:T(8,128)(2,1)} %bitcast.16, bf16[2,27,8,256]{3,2,1,0:T(8,128)(2,1)} %bitcast.19, f32[2,27,8,256]{3,2,1,0:T(8,128)} %bitcast.11, ...), custom_call_target="tpu_custom_call" | custom-call | tf_op jit(solution)/shard_map/pallas_call | solution.py:368
  103.2 0.0 copy-start.2
  103.2 0.0 copy-start.1
  103.2 1.2 %copy.10 = bf16[1,2,216,256]{3,1,2,0:T(2,128)(2,1)S(1)} copy(bf16[1,2,216,256]{3,2,1,0:T(8,128)(2,1)} %bitcast.20) | data formatting | bytes 442368
  104.4 0.6 dynamic-slice_convert_fusion
  105.0 0.0 copy-done.2
  105.0 0.7 copy.14
  105.7 0.0 copy-done.1
  105.7 0.0 copy-start
  105.7 0.8 copy.15
  106.5 0.4 copy-done
  106.9 0.8 copy.16
Async XLA Ops:
  103.2 1.8 %copy-start.2 = (bf16[8,4,16,256]{3,2,1,0:T(8,128)(2,1)S(1)}, bf16[8,4,16,256]{3,2,1,0:T(8,128)(2,1)}, u32[]{:S(2)}) copy-start(bf16[8,4,16,256]{3,2,1,0:T(8,128)(2,1)} %get-tuple-element.8) | copy-start | bytes 786436
  103.2 2.5 %copy-start.1 = (f32[2,27,8,256]{3,2,1,0:T(8,128)S(1)}, f32[2,27,8,256]{3,2,1,0:T(8,128)}, u32[]{:S(2)}) copy-start(f32[2,27,8,256]{3,2,1,0:T(8,128)} %get-tuple-element.10) | copy-start | bytes 1327108
  105.7 1.2 %copy-start = (f32[2,27,8,256]{3,2,1,0:T(8,128)S(1)}, f32[2,27,8,256]{3,2,1,0:T(8,128)}, u32[]{:S(2)}) copy-start(f32[2,27,8,256]{3,2,1,0:T(8,128)} %get-tuple-element.11) | copy-start | bytes 1327108

commit v2 on v1

v2 whole, which is shorter than its diff:
```python
import jax
import jax.numpy as jnp
from jax import lax
from jax.experimental import pallas as pl
from jax.experimental.pallas import tpu as pltpu
from jax.sharding import PartitionSpec as P

MESH = pl.DeviceIdType.MESH
F32 = jnp.float32
BF16 = jnp.bfloat16
UNITS = 27
ZS = 16
NX = 5
N_A2A, N_HALO, N_RING, N_SIB, N_G = 7, 6, 48, 24, 8


def unit_of(row_unit):
    panel, within = divmod(row_unit, UNITS)
    group, place = divmod(within, 7)
    return panel // ZS, panel % ZS, group // 2, group % 2, place


def runs_of(chunk):
    runs = []
    for k in range(96):
        at = unit_of(96 * chunk + k)
        if runs and runs[-1][1][:4] == at[:4] and runs[-1][1][4] + runs[-1][2] == at[4]:
            runs[-1][2] += 1
        else:
            runs.append([k, at, 1])
    return runs


def gelu(v):
    return 0.5 * v * (1.0 + jnp.tanh(0.7978845608028654 * (v + 0.044715 * (v * v * v))))


def body(
    owner, vol, grads, master, mom1, mom2,
    conv, pan, sums,
    stage, paired, got, gsum, gall, filt, raw, edge_out, edge_in, field, acc, hid, wbuf,
    bar_send, bar_recv,
):
    s = lax.axis_index("space")
    r = lax.axis_index("rep")
    yhi, z = s // ZS, lax.rem(s, ZS)
    ylo, x, c = r // 8, lax.rem(r // 2, 4), lax.rem(r, 2)
    y = 2 * yhi + ylo
    bx, by, bz = s // 4, lax.rem(s // 2, 2), lax.rem(s, 2)

    def device(px, py, pz, pc):
        return (py // 2 * ZS + pz, lax.rem(py, 2) * 8 + 2 * px + pc)

    q = 4 * ylo + x
    xp, xm, xo = lax.rem(x + 1, 4), lax.rem(x + 3, 4), lax.rem(x + 2, 4)
    yp, ym, yo = lax.rem(y + 1, 4), lax.rem(y + 3, 4), lax.rem(y + 2, 4)
    zh, zl = z // 4, lax.rem(z, 4)
    lp, lm, lo = lax.rem(zl + 1, 4), lax.rem(zl + 3, 4), lax.rem(zl + 2, 4)

    def along_z(n):
        return device(x, y, lax.rem(z + n + ZS, ZS), c)

    sib_dev = device(x, y, z, 1 - c)
    other_y = jnp.where(ylo == 0, ym, yp)

    def chip(n):
        return (s, 2 * n + c)

    flip = 2 - 4 * by
    halo_peers = []
    for dx, fl in ((-1, 0), (1, 0), (0, 1), (-1, 1), (1, 1)):
        halo_peers.append((dx, fl, (lax.rem(s + fl * flip + 4 * dx + 32, 32), r)))

    barrier = pltpu.get_barrier_semaphore()
    all_peers = [sib_dev] + [chip(lax.rem(q + d, 8)) for d in range(1, 8)]
    all_peers += [along_z(n) for n in (4, -4, 8, 1, -1, 2, -2)] + [device(x, other_y, z, c)]
    all_peers += [p for _, _, p in halo_peers]
    for p in all_peers:
        pl.semaphore_signal(barrier, inc=1, device_id=p, device_id_type=MESH)

    for d in range(16):
        dc, dl, dx = d // 8, d // 4 % 2, d % 4
        first = 7 * (2 * dc + dl) + 2 * dx
        for u in range(2):
            at = min(first + (u if dx < 3 else 0), UNITS - 1)
            stage[dc, d % 8, :, 0, u] = grads[:, at]
            stage[dc, d % 8, :, 1, u] = mom1[:, at].astype(BF16)
            stage[dc, d % 8, :, 2, u] = mom2[:, at].astype(BF16)

    pl.semaphore_wait(barrier, len(all_peers))

    sent = []
    base = [0]

    def take(n):
        base[0] += n
        return base[0] - n

    def send(src, dst, k, dev):
        copy = pltpu.make_async_remote_copy(
            src_ref=src, dst_ref=dst, send_sem=bar_send.at[k], recv_sem=bar_recv.at[k],
            device_id=dev, device_id_type=MESH,
        )
        copy.start()
        sent.append(copy)

    def arrived(dst, k):
        pltpu.make_async_remote_copy(
            src_ref=dst, dst_ref=dst, send_sem=bar_send.at[k], recv_sem=bar_recv.at[k],
            device_id=(s, r), device_id_type=MESH,
        ).wait_recv()

    pair = take(1)
    send(stage.at[1 - c], paired, pair, sib_dev)
    halo = take(N_HALO)
    x_src = {-1: (0, 2), 0: (0, 8), 1: (6, 2)}
    x_dst = {-1: 10, 0: 2, 1: 0}
    for k, (dx, fl, dev) in enumerate(halo_peers):
        sx, nx = x_src[dx]
        sy, dy, ny = (2 * (1 - by), 6 * by, 2) if fl else (0, 2, 4)
        send(
            vol.at[pl.ds(sx, nx), pl.ds(sy, ny)],
            raw.at[pl.ds(x_dst[dx], nx), pl.ds(dy, ny)],
            halo + k, dev,
        )

    arrived(paired, pair)
    a2a = take(N_A2A)
    sib_owns = [owner[f, s] == 2 * q + 1 - c for f in range(2)]
    for d in range(1, 9):
        to = lax.rem(q + d, 8)
        for f in range(2):
            g = stage[c, to, f, 0].astype(F32) + paired[to, f, 0].astype(F32)
            stage[c, to, f, 0] = g.astype(BF16)
            for k in (1, 2):
                mine, other = stage[c, to, f, k], paired[to, f, k]
                stage[c, to, f, k] = jnp.where(sib_owns[f], other.astype(F32), mine.astype(F32)).astype(BF16)
        if d < 8:
            send(stage.at[c, to], got.at[q], a2a + d - 1, chip(to))
    got[q] = stage[c, q]
    raw[2:10, 2:6] = vol[...]

    for d in range(1, 8):
        arrived(got.at[lax.rem(q + 8 - d, 8)], a2a + d - 1)
    first = 7 * (2 * c + ylo) + 2 * x
    corr_one = 1.0 - 0.9**10
    corr_two = 1.0 - 0.95**10
    for f in range(2):
        own = owner[f, s] // 2
        for u in range(2):
            total = got[0, f, 0, u].astype(F32)
            for k in range(1, 8):
                total = total + got[k, f, 0, u].astype(F32)
            m_new = 0.9 * got[own, f, 1, u].astype(F32) + 0.1 * total
            v_new = 0.95 * got[own, f, 2, u].astype(F32) + 0.05 * (total * total)
            w = master[f, jnp.minimum(first + u, UNITS - 1)]
            step = m_new / corr_one / (jnp.sqrt(v_new / corr_two) + 1e-08) + 0.1 * w
            gsum[f, u] = total.astype(BF16)
            filt[f, yhi, 0, 0, c, ylo, 2 * x + u] = (w - 0.004 * step).astype(BF16)

    mine = pl.ds(2 * x, 2)

    def blk(off, k):
        return filt.at[:, yhi, off, k, c, ylo, mine]

    far = take(3)
    send(blk(0, 0), blk(3, 0), far, along_z(4))
    send(blk(0, 0), blk(1, 0), far + 1, along_z(-4))
    send(blk(0, 0), blk(2, 0), far + 2, along_z(8))
    near = {off: take(3) for off in (0, 3, 2)}

    def send_near(off):
        send(blk(off, 0), blk(off, 3), near[off], along_z(1))
        send(blk(off, 0), blk(off, 1), near[off] + 1, along_z(-1))
        send(blk(off, 0), blk(off, 2), near[off] + 2, along_z(2 - 4 * yhi))

    def wait_near(off):
        for n, k in enumerate((3, 1, 2)):
            arrived(blk(off, k), near[off] + n)

    side = take(3)

    def side_block(pos):
        return filt.at[:, yhi, 1, 0, c, ylo, pl.ds(2 * pos, 2)]

    kinds = {
        (0, 0): 1, (1, 0): 0, (0, 3): 0, (1, 3): 1, (0, 2): 1, (1, 2): 0, (0, 1): 2, (1, 1): 2,
    }
    ring = take(N_RING + 16)
    sib = take(N_SIB + 8)
    ways = {
        "x": (x, xp, xm, xo, device(xp, y, z, c), device(xm, y, z, c)),
        "y": (y, yp, ym, yo, device(x, yp, z, c), device(x, ym, z, c)),
        "z": (0, 1, 3, 2, along_z(1), along_z(-1)),
    }
    order = {0: "yx", 1: "xy", 2: "yz"}

    def ring_of(f, off, phase):
        n = ring + 4 * (8 * f + 2 * off + phase)
        kind = kinds[f, off]

        def reg(pos, half=None, core=c):
            if kind == 2:
                if phase == 0:
                    u0, nu = {None: (0, 7), 0: (0, 4), 1: (4, 3)}[half]
                    return filt.at[f, pos // 2, off, 0, core, lax.rem(pos, 2), pl.ds(u0, nu)]
                hi = pl.ds(0, 2) if half is None else pl.ds(half, 1)
                return filt.at[f, hi, off, pos, core, :, pl.ds(0, 7)]
            ks = pl.ds(0, 4) if half is None else pl.ds(2 * half, 2)
            if kind == 0 and phase == 0:
                return filt.at[f, pos // 2, off, ks, core, lax.rem(pos, 2), mine]
            if kind == 0:
                hi = pl.ds(0, 2) if half is None else pl.ds(half, 1)
                return filt.at[f, hi, off, :, core, :, pl.ds(2 * pos, 2)]
            if phase == 0:
                return filt.at[f, yhi, off, ks, core, ylo, pl.ds(2 * pos, 2)]
            return filt.at[f, pos // 2, off, ks, core, lax.rem(pos, 2), pl.ds(0, 7)]

        return (n, order[kind][phase] == "z") + ways[order[kind][phase]] + (reg,)

    def start(f, off, phase):
        n, rel, me, plus, minus, opp, to_plus, to_minus, reg = ring_of(f, off, phase)
        send(reg(me), reg(minus if rel else me), n, to_plus)
        send(reg(me), reg(plus if rel else me), n + 1, to_minus)
        if phase == 1:
            send(reg(me), reg(me), sib + 4 * (4 * f + off), sib_dev)

    def turn(f, off, phase):
        n, rel, me, plus, minus, opp, to_plus, to_minus, reg = ring_of(f, off, phase)
        arrived(reg(minus), n)
        send(reg(minus, 0), reg(opp if rel else minus, 0), n + 2, to_plus)
        arrived(reg(plus), n + 1)
        send(reg(plus, 1), reg(opp if rel else plus, 1), n + 3, to_minus)
        if phase == 1:
            m = sib + 4 * (4 * f + off)
            send(reg(minus), reg(minus), m + 1, sib_dev)
            send(reg(plus), reg(plus), m + 2, sib_dev)

    def end(f, off, phase):
        n, rel, me, plus, minus, opp, to_plus, to_minus, reg = ring_of(f, off, phase)
        arrived(reg(opp, 0), n + 2)
        arrived(reg(opp, 1), n + 3)
        if phase == 1:
            send(reg(opp), reg(opp), sib + 4 * (4 * f + off) + 3, sib_dev)

    def from_sib(f):
        for off in range(4):
            n, rel, me, plus, minus, opp, to_plus, to_minus, reg = ring_of(f, off, 1)
            for m, pos in enumerate((me, minus, plus, opp)):
                arrived(reg(pos, None, 1 - c), sib + 4 * (4 * f + off) + m)

    send_near(0)
    wait_near(0)
    start(0, 0, 0)
    start(1, 0, 0)
    arrived(blk(3, 0), far)
    send_near(3)
    arrived(blk(1, 0), far + 1)
    for n, pos in enumerate((xp, xm, xo)):
        send(side_block(x), side_block(x), side + n, device(pos, y, z, c))
    arrived(blk(2, 0), far + 2)
    send_near(2)
    turn(0, 0, 0)
    turn(1, 0, 0)
    wait_near(3)
    start(0, 3, 0)
    start(1, 3, 0)
    for n, pos in enumerate((xm, xp, xo)):
        arrived(side_block(pos), side + n)
    start(0, 1, 0)
    start(1, 1, 0)

    for k, (dx, fl, dev) in enumerate(halo_peers):
        sx, nx = x_src[dx]
        dy, ny = (6 * (1 - by), 2) if fl else (2, 4)
        dst_x = {-1: 0, 0: 2, 1: 10}[dx]
        pairs = raw.at[pl.ds(dst_x, nx), pl.ds(dy, ny)]
        arrived(pairs, halo + {0: 1, 1: 0, 2: 2, 3: 4, 4: 3}[k])

    def pack(i, carry):
        rows = [raw[i, j].astype(F32) for j in range(8)]
        near = jnp.concatenate([jnp.where(bz == 0, v[15:16], v[0:1]) for v in rows], axis=0)
        far = jnp.concatenate([jnp.where(bz == 0, v[14:15], v[1:2]) for v in rows], axis=0)
        edge_out[i] = jnp.concatenate([near, far], axis=0).astype(BF16)
        return carry

    lax.fori_loop(0, 12, pack, 0)
    z_partner = z + 1 - 2 * bz
    send(edge_out, edge_in, halo + 5, device(x, y, z_partner, c))

    end(0, 0, 0)
    start(0, 0, 1)
    wait_near(2)
    start(0, 2, 0)
    start(1, 2, 0)
    turn(0, 3, 0)
    turn(0, 1, 0)
    turn(1, 3, 0)
    turn(1, 1, 0)
    end(1, 0, 0)
    end(0, 3, 0)
    start(0, 3, 1)
    turn(0, 2, 0)
    turn(1, 2, 0)
    end(0, 1, 0)
    start(0, 1, 1)
    end(0, 2, 0)
    start(0, 2, 1)
    turn(0, 0, 1)
    start(1, 0, 1)
    for off in (3, 1, 2):
        end(1, off, 0)
        start(1, off, 1)

    gs = take(N_G)
    for d in range(1, 8):
        to = lax.rem(q + d, 8)
        send(gsum, gall.at[c, q], gs + d - 1, chip(to))
    gall[c, q] = gsum[...]

    arrived(edge_in, halo + 5)

    def shifts(i, carry):
        edges = edge_in[i].astype(F32)
        x_ok = (i + 8 * bx >= 2) & (i + 8 * bx < 66)
        for j in range(8):
            y_ok = (j + 4 * by >= 2) & (j + 4 * by < 10)
            ok = x_ok & y_ok
            v = jnp.where(ok, raw[i, j].astype(F32), 0.0)
            e0 = jnp.where(ok, edges[j : j + 1], 0.0)
            e1 = jnp.where(ok, edges[8 + j : 9 + j], 0.0)
            none = jnp.zeros((1, 256), F32)
            rest = jnp.zeros((7, 256), F32)
            low = bz == 0
            field[i, j, :, 0:256] = jnp.concatenate(
                [jnp.where(low, none, e0), v[0:15], jnp.where(low, v[15:16], e1), rest], axis=0
            ).astype(BF16)
            field[i, j, :, 256:512] = jnp.concatenate([v, e0, rest], axis=0).astype(BF16)
            field[i, j, :, 512:768] = jnp.concatenate(
                [v[1:16], jnp.where(low, e0, none), jnp.where(low, e1, v[0:1]), rest], axis=0
            ).astype(BF16)
        return carry

    lax.fori_loop(0, 12, shifts, 0)

    for off in (3, 1, 2):
        turn(0, off, 1)
    end(0, 0, 1)
    turn(1, 0, 1)
    turn(1, 3, 1)
    for off in (3, 1, 2):
        end(0, off, 1)
    from_sib(0)

    def load_chunk(f, n):
        for at, (a, b, cc, d, u), count in runs_of(n):
            k = lax.rem(b - z + ZS, 4)
            step = k - 4 * (k // (2 + a))
            off = lax.rem(b - z - step + 2 * ZS, ZS) // 4
            wbuf[at : at + count] = filt[f, a, off, k, cc, d, u : u + count]

    y_at = 1 - by

    def first_conv(n):
        a, b = divmod(n, 3)
        load_chunk(0, n)

        def one(i, carry):
            lhs = field[pl.ds(NX * i + a, NX), pl.ds(y_at + b, 5)].reshape(NX * 120, 768)
            part = jnp.dot(lhs, wbuf[...].reshape(768, 256), preferred_element_type=F32)
            rows = pl.ds(NX * i, NX)
            part = part.reshape(NX, 5, 24, 256)
            acc[rows] = part if n == 0 else acc[rows] + part
            return carry

        lax.fori_loop(0, 10 // NX, one, 0)

    first_conv(0)
    first_conv(1)
    turn(1, 1, 1)
    turn(1, 2, 1)
    for n in range(2, 5):
        first_conv(n)
    for off in (0, 3, 1, 2):
        end(1, off, 1)
    for d in range(1, 8):
        arrived(gall.at[c, lax.rem(q + 8 - d, 8)], gs + d - 1)
    send(gall.at[c], gall.at[c], gs + 7, sib_dev)
    for n in range(5, 9):
        first_conv(n)

    def activate(i, carry):
        ok = (i + 8 * bx >= 1) & (i + 8 * bx < 65)
        low = bz == 0
        hid[i, 5 * by] = jnp.zeros((16, 768), BF16)
        for j in range(5):
            h = jnp.where(ok, gelu(acc[i, j]), 0.0)
            none = jnp.zeros((1, 256), F32)
            edge = h[16:17]
            hid[i, y_at + j, :, 0:256] = jnp.concatenate(
                [jnp.where(low, none, edge), h[0:15]], axis=0
            ).astype(BF16)
            hid[i, y_at + j, :, 256:512] = h[0:16].astype(BF16)
            hid[i, y_at + j, :, 512:768] = jnp.concatenate(
                [h[1:16], jnp.where(low, edge, none)], axis=0
            ).astype(BF16)
        return carry

    lax.fori_loop(0, 10, activate, 0)

    from_sib(1)
    for n in range(9):
        a, b = divmod(n, 3)
        load_chunk(1, n)
        lhs = hid[a : a + 8, b : b + 4].reshape(512, 768)
        part = jnp.dot(lhs, wbuf[...].reshape(768, 256), preferred_element_type=F32)
        part = part.reshape(8, 4, 16, 256)
        conv[...] = part if n == 0 else conv[...] + part

    arrived(gall.at[1 - c], gs + 7)
    sums[...] = gall[...]
    for f in range(2):
        for g in range(4):
            n = min(7, UNITS - 7 * g)
            pan[f, 7 * g : 7 * g + n] = filt[f, yhi, 0, 0, g // 2, g % 2, 0:n]
    for copy in sent:
        copy.wait_send()


def outputs(owned, conv, gall, mom1, mom2, feat, mom1_out, mom2_out):
    def finish(i, carry):
        feat[i] = gelu(conv[i]).astype(BF16)
        return carry

    lax.fori_loop(0, 8, finish, 0)
    for f in range(2):
        here = owned[f] == 1
        for d in range(16):
            dc, dl, dx = d // 8, d // 4 % 2, d % 4
            for u in range(2):
                at = 7 * (2 * dc + dl) + 2 * dx + u
                if 2 * dx + u > 6 or at >= UNITS:
                    continue
                g = gall[dc, d % 8, f, u].astype(F32)
                m, v = mom1[f, at], mom2[f, at]
                mom1_out[f, at] = jnp.where(here, 0.9 * m + 0.1 * g, m)
                mom2_out[f, at] = jnp.where(here, 0.95 * v + 0.05 * (g * g), v)


def shards(volumes, grad_parts, master, mom1, mom2, owner):
    def units(a):
        return a.reshape(2, UNITS, 8, 256)

    vmem = pl.BlockSpec(memory_space=pltpu.VMEM)
    n_sems = 16 + N_A2A + N_HALO + N_RING + 16 + N_SIB + 8 + N_G
    state = jax.ShapeDtypeStruct((2, UNITS, 8, 256), F32)
    smem = pl.BlockSpec(memory_space=pltpu.SMEM)
    args = (units(mom1[0]), units(mom2[0]))
    conv, pan, gall = pl.pallas_call(
        body,
        out_shape=(
            jax.ShapeDtypeStruct((8, 4, 16, 256), F32),
            jax.ShapeDtypeStruct((2, UNITS, 8, 256), BF16),
            jax.ShapeDtypeStruct((2, 8, 2, 2, 8, 256), BF16),
        ),
        in_specs=[smem] + [vmem] * 5,
        out_specs=[vmem] * 3,
        scratch_shapes=[
            pltpu.VMEM((2, 8, 2, 3, 2, 8, 256), BF16),
            pltpu.VMEM((8, 2, 3, 2, 8, 256), BF16),
            pltpu.VMEM((8, 2, 3, 2, 8, 256), BF16),
            pltpu.VMEM((2, 2, 8, 256), BF16),
            pltpu.VMEM((2, 8, 2, 2, 8, 256), BF16),
            pltpu.VMEM((2, 2, 4, 4, 2, 2, 8, 8, 256), BF16),
            pltpu.VMEM((12, 8, 16, 256), BF16),
            pltpu.VMEM((12, 16, 256), BF16),
            pltpu.VMEM((12, 16, 256), BF16),
            pltpu.VMEM((12, 8, 24, 768), BF16),
            pltpu.VMEM((10, 5, 24, 256), F32),
            pltpu.VMEM((10, 6, 16, 768), BF16),
            pltpu.VMEM((96, 8, 256), BF16),
            pltpu.SemaphoreType.DMA((n_sems,)),
            pltpu.SemaphoreType.DMA((n_sems,)),
        ],
        compiler_params=pltpu.CompilerParams(
            collective_id=0, has_side_effects=True, vmem_limit_bytes=56 << 20
        ),
    )(owner, volumes[0, 0], units(grad_parts[0]), units(master), *args)
    s, r = lax.axis_index("space"), lax.axis_index("rep")
    owned = (lax.dynamic_slice_in_dim(owner, s, 1, 1)[:, 0] == r).astype(jnp.int32)
    feat, m_out, v_out = pl.pallas_call(
        outputs,
        out_shape=(jax.ShapeDtypeStruct((8, 4, 16, 256), BF16), state, state),
        in_specs=[smem] + [vmem] * 4,
        out_specs=[vmem] * 3,
        compiler_params=pltpu.CompilerParams(vmem_limit_bytes=16 << 20),
    )(owned, conv, gall, *args)
    rows = lax.dynamic_slice_in_dim(pan.reshape(2, 216, 256), 27 * (r // 2), 27, 1)
    rows = rows.astype(F32).reshape(2, 2, 3456)
    share = lax.dynamic_index_in_dim(rows, lax.rem(r, 2), 1, keepdims=False)
    return (
        feat[None, None],
        share,
        m_out.reshape(1, 2, 216, 256),
        v_out.reshape(1, 2, 216, 256),
    )


def solution(mesh):
    placed = (
        P("rep", "space", None, None, None, None),
        P("rep", None, "space", None),
        P(None, "space", None),
        P("rep", None, "space", None),
        P("rep", None, "space", None),
        P(),
    )
    return jax.shard_map(
        shards,
        mesh=mesh,
        in_specs=placed,
        out_specs=(
            P("rep", "space", None, None, None, None),
            P(None, ("space", "rep")),
            P("rep", None, "space", None),
            P("rep", None, "space", None),
        ),
        check_vma=False,
    )
```

time: 109 us -> 88.2 us (0.81); the launches traced: 108 us -> 88 us
  Pallas kernels: 103 us -> 83.8 us
  local copies, waits for them, and re-layouts: 3.82 us -> 2.42 us
    pallas_call x1 -> x2, Pallas kernels: 103 us -> 83.8 us  [the longest x1 82 us: shards(): pl.pallas_call(body, out_shape=(jax.ShapeDtypeStruct((8, 4, 16, 256), F32...]
    unnamed x10 -> x11, local copies, waits for them, and re-layouts: 3.82 us -> 2.35 us
where the time goes in v2:
time: 88.2 us; the launch traced here: 88 us
  Pallas kernels  83.8 us (95%)
  local copies, waits for them, and re-layouts  2.42 us (3%)
  other arithmetic  1.03 us (1%)
    pallas_call x1, Pallas kernels, shards(): pl.pallas_call(body, out_shape=(jax.ShapeDtypeStruct((8, 4, 16, 256), F32...  82 us
    unnamed x11, local copies, waits for them, and re-layouts  2.35 us
    pallas_call x1, Pallas kernels, shards(): pl.pallas_call(outputs, out_shape=(jax.ShapeDtypeStruct((8, 4, 16, 256),...  1.78 us

profile of v2, /device:TPU:1, one launch (start us, length us, event | category | flops | bytes accessed | tf_op | source)
XLA Modules:
  0.0 88.0 jit_solution(11455318276498358322)
XLA Ops:
  0.7 0.0 copy-start.4
  0.7 0.7 copy-done.4
  1.3 0.2 fusion.owned
  1.5 0.0 copy-start
  1.5 0.0 copy-start.1
  1.5 82.0 %shard_map.93 = (f32[8,4,16,256]{3,2,1,0:T(8,128)}, bf16[2,27,8,256]{3,2,1,0:T(8,128)(2,1)}, bf16[2,8,2,2,8,256]{5,4,3,2,1,0:T(8,128)(2,1)}) custom-call(s32[2,32]{1,0:T(2,128)} %owner.1, bf16[8,4,16,256]{3,2,1,0:T(8,128)(2,1)} %bitcast.17, bf16[2,27,8,256]{3,2,1,0:T(8,128)(2,1)} %bitcast.18, f32[2,27,8,256]{3,2,1,0:T(8,128)} %bitcast.16, ...), custom_call_target="tpu_custom_call" | custom-call | tf_op jit(solution)/shard_map/pallas_call | solution.py:459
  83.6 0.0 copy-start.3
  83.6 0.8 dynamic-slice_convert_fusion
  84.5 0.6 copy.13
  85.1 0.0 copy-done
  85.1 0.0 copy-done.1
  85.1 0.0 copy-done.3
  85.1 0.0 copy-start.2
  85.2 1.0 %copy-done.2 = f32[8,4,16,256]{3,2,1,0:T(8,128)S(1)} copy-done((f32[8,4,16,256]{3,2,1,0:T(8,128)S(1)}, f32[8,4,16,256]{3,2,1,0:T(8,128)}, u32[]{:S(2)}) %copy-start.2) | copy-done | bytes 524312
  86.2 1.8 %shard_map.94 = (bf16[8,4,16,256]{3,2,1,0:T(8,128)(2,1)}, f32[2,27,8,256]{3,2,1,0:T(8,128)}, f32[2,27,8,256]{3,2,1,0:T(8,128)}) custom-call(s32[2]{0:T(128)S(1)} %fusion.owned, f32[8,4,16,256]{3,2,1,0:T(8,128)S(1)} %copy-done.2, bf16[2,8,2,2,8,256]{5,4,3,2,1,0:T(8,128)(2,1)S(1)} %copy-done.3, f32[2,27,8,256]{3,2,1,0:T(8,128)S(1)} %bitcast.13, ...), custom_call_target="tpu_custom_call" | custom-call | tf_op jit(solution)/shard_map/pallas_call | solution.py:491
  (2 shorter events, 0.1 us)
Async XLA Ops:
  0.7 0.7 copy-start.4
  1.5 83.6 %copy-start = (f32[1,2,216,256]{3,2,1,0:T(8,128)S(1)}, f32[1,2,216,256]{3,2,1,0:T(8,128)}, u32[]{:S(2)}) copy-start(f32[1,2,216,256]{3,2,1,0:T(8,128)} %param.9) | copy-start | bytes 1327108
  1.5 83.6 %copy-start.1 = (f32[1,2,216,256]{3,2,1,0:T(8,128)S(1)}, f32[1,2,216,256]{3,2,1,0:T(8,128)}, u32[]{:S(2)}) copy-start(f32[1,2,216,256]{3,2,1,0:T(8,128)} %param.10) | copy-start | bytes 1327108
  83.6 1.6 %copy-start.3 = (bf16[2,8,2,2,8,256]{5,4,3,2,1,0:T(8,128)(2,1)S(1)}, bf16[2,8,2,2,8,256]{5,4,3,2,1,0:T(8,128)(2,1)}, u32[]{:S(2)}) copy-start(bf16[2,8,2,2,8,256]{5,4,3,2,1,0:T(8,128)(2,1)} %get-tuple-element.11.gall) | copy-start | bytes 786436
  85.1 1.0 %copy-start.2 = (f32[8,4,16,256]{3,2,1,0:T(8,128)S(1)}, f32[8,4,16,256]{3,2,1,0:T(8,128)}, u32[]{:S(2)}) copy-start(f32[8,4,16,256]{3,2,1,0:T(8,128)} %get-tuple-element.10.conv) | copy-start | bytes 1572868

commit v3 on v2

--- a/solution.py
+++ b/solution.py
@@ -12,6 +12,17 @@
 ZS = 16
 NX = 5
 N_A2A, N_HALO, N_RING, N_SIB, N_G = 7, 6, 48, 24, 8
+
+PLAN = (
+    ("near", 0, 0), ("far", 0, 1), ("far", 0, 3), ("turn0", 0, 0), ("turn0", 1, 0), ("side", 0, 1), ("end0", 0, 0),
+    ("far", 0, 2), ("near", 0, 3), ("turn0", 0, 1), ("turn0", 1, 1), ("turn0", 1, 3), ("near", 0, 2), ("edges",),
+    ("end0", 1, 0), ("turn1", 0, 0), ("turn0", 0, 3), ("turn0", 1, 2), ("turn0", 0, 2), ("end1", 0, 0),
+    ("end0", 0, 3), ("end0", 0, 1), ("end0", 1, 3), ("end0", 0, 2), ("turn1", 1, 0), ("end0", 1, 1), ("turn1", 0, 3),
+    ("turn1", 0, 1), ("shift",), ("end0", 1, 2), ("sums",), ("turn1", 0, 2), ("end1", 0, 1), ("end1", 0, 3),
+    ("turn1", 1, 3), ("turn1", 1, 1), ("end1", 0, 2), ("end1", 1, 0), ("turn1", 1, 2), ("sib", 0), ("conv", 0),
+    ("conv", 1), ("end1", 1, 3), ("end1", 1, 1), ("end1", 1, 2), ("conv", 2), ("conv", 3), ("conv", 4), ("gs",),
+    ("conv", 5), ("conv", 6), ("conv", 7), ("conv", 8),
+)
 
 
 def unit_of(row_unit):
@@ -249,108 +260,58 @@
             for m, pos in enumerate((me, minus, plus, opp)):
                 arrived(reg(pos, None, 1 - c), sib + 4 * (4 * f + off) + m)
 
-    send_near(0)
-    wait_near(0)
-    start(0, 0, 0)
-    start(1, 0, 0)
-    arrived(blk(3, 0), far)
-    send_near(3)
-    arrived(blk(1, 0), far + 1)
-    for n, pos in enumerate((xp, xm, xo)):
-        send(side_block(x), side_block(x), side + n, device(pos, y, z, c))
-    arrived(blk(2, 0), far + 2)
-    send_near(2)
-    turn(0, 0, 0)
-    turn(1, 0, 0)
-    wait_near(3)
-    start(0, 3, 0)
-    start(1, 3, 0)
-    for n, pos in enumerate((xm, xp, xo)):
-        arrived(side_block(pos), side + n)
-    start(0, 1, 0)
-    start(1, 1, 0)
-
-    for k, (dx, fl, dev) in enumerate(halo_peers):
-        sx, nx = x_src[dx]
-        dy, ny = (6 * (1 - by), 2) if fl else (2, 4)
-        dst_x = {-1: 0, 0: 2, 1: 10}[dx]
-        pairs = raw.at[pl.ds(dst_x, nx), pl.ds(dy, ny)]
-        arrived(pairs, halo + {0: 1, 1: 0, 2: 2, 3: 4, 4: 3}[k])
-
-    def pack(i, carry):
-        rows = [raw[i, j].astype(F32) for j in range(8)]
-        near = jnp.concatenate([jnp.where(bz == 0, v[15:16], v[0:1]) for v in rows], axis=0)
-        far = jnp.concatenate([jnp.where(bz == 0, v[14:15], v[1:2]) for v in rows], axis=0)
-        edge_out[i] = jnp.concatenate([near, far], axis=0).astype(BF16)
-        return carry
-
-    lax.fori_loop(0, 12, pack, 0)
-    z_partner = z + 1 - 2 * bz
-    send(edge_out, edge_in, halo + 5, device(x, y, z_partner, c))
-
-    end(0, 0, 0)
-    start(0, 0, 1)
-    wait_near(2)
-    start(0, 2, 0)
-    start(1, 2, 0)
-    turn(0, 3, 0)
-    turn(0, 1, 0)
-    turn(1, 3, 0)
-    turn(1, 1, 0)
-    end(1, 0, 0)
-    end(0, 3, 0)
-    start(0, 3, 1)
-    turn(0, 2, 0)
-    turn(1, 2, 0)
-    end(0, 1, 0)
-    start(0, 1, 1)
-    end(0, 2, 0)
-    start(0, 2, 1)
-    turn(0, 0, 1)
-    start(1, 0, 1)
-    for off in (3, 1, 2):
-        end(1, off, 0)
-        start(1, off, 1)
-
     gs = take(N_G)
-    for d in range(1, 8):
-        to = lax.rem(q + d, 8)
-        send(gsum, gall.at[c, q], gs + d - 1, chip(to))
-    gall[c, q] = gsum[...]
-
-    arrived(edge_in, halo + 5)
-
-    def shifts(i, carry):
-        edges = edge_in[i].astype(F32)
-        x_ok = (i + 8 * bx >= 2) & (i + 8 * bx < 66)
-        for j in range(8):
-            y_ok = (j + 4 * by >= 2) & (j + 4 * by < 10)
-            ok = x_ok & y_ok
-            v = jnp.where(ok, raw[i, j].astype(F32), 0.0)
-            e0 = jnp.where(ok, edges[j : j + 1], 0.0)
-            e1 = jnp.where(ok, edges[8 + j : 9 + j], 0.0)
-            none = jnp.zeros((1, 256), F32)
-            rest = jnp.zeros((7, 256), F32)
-            low = bz == 0
-            field[i, j, :, 0:256] = jnp.concatenate(
-                [jnp.where(low, none, e0), v[0:15], jnp.where(low, v[15:16], e1), rest], axis=0
-            ).astype(BF16)
-            field[i, j, :, 256:512] = jnp.concatenate([v, e0, rest], axis=0).astype(BF16)
-            field[i, j, :, 512:768] = jnp.concatenate(
-                [v[1:16], jnp.where(low, e0, none), jnp.where(low, e1, v[0:1]), rest], axis=0
-            ).astype(BF16)
-        return carry
-
-    lax.fori_loop(0, 12, shifts, 0)
-
-    for off in (3, 1, 2):
-        turn(0, off, 1)
-    end(0, 0, 1)
-    turn(1, 0, 1)
-    turn(1, 3, 1)
-    for off in (3, 1, 2):
-        end(0, off, 1)
-    from_sib(0)
+
+    def edges():
+        for k, (dx, fl, dev) in enumerate(halo_peers):
+            sx, nx = x_src[dx]
+            dy, ny = (6 * (1 - by), 2) if fl else (2, 4)
+            dst_x = {-1: 0, 0: 2, 1: 10}[dx]
+            pairs = raw.at[pl.ds(dst_x, nx), pl.ds(dy, ny)]
+            arrived(pairs, halo + {0: 1, 1: 0, 2: 2, 3: 4, 4: 3}[k])
+
+        def pack(i, carry):
+            rows = [raw[i, j].astype(F32) for j in range(8)]
+            near = jnp.concatenate([jnp.where(bz == 0, v[15:16], v[0:1]) for v in rows], axis=0)
+            far = jnp.concatenate([jnp.where(bz == 0, v[14:15], v[1:2]) for v in rows], axis=0)
+            edge_out[i] = jnp.concatenate([near, far], axis=0).astype(BF16)
+            return carry
+
+        lax.fori_loop(0, 12, pack, 0)
+        z_partner = z + 1 - 2 * bz
+        send(edge_out, edge_in, halo + 5, device(x, y, z_partner, c))
+
+    def send_sums():
+        for d in range(1, 8):
+            to = lax.rem(q + d, 8)
+            send(gsum, gall.at[c, q], gs + d - 1, chip(to))
+        gall[c, q] = gsum[...]
+
+    def shift_field():
+        arrived(edge_in, halo + 5)
+
+        def shifts(i, carry):
+            edges = edge_in[i].astype(F32)
+            x_ok = (i + 8 * bx >= 2) & (i + 8 * bx < 66)
+            for j in range(8):
+                y_ok = (j + 4 * by >= 2) & (j + 4 * by < 10)
+                ok = x_ok & y_ok
+                v = jnp.where(ok, raw[i, j].astype(F32), 0.0)
+                e0 = jnp.where(ok, edges[j : j + 1], 0.0)
+                e1 = jnp.where(ok, edges[8 + j : 9 + j], 0.0)
+                none = jnp.zeros((1, 256), F32)
+                rest = jnp.zeros((7, 256), F32)
+                low = bz == 0
+                field[i, j, :, 0:256] = jnp.concatenate(
+                    [jnp.where(low, none, e0), v[0:15], jnp.where(low, v[15:16], e1), rest], axis=0
+                ).astype(BF16)
+                field[i, j, :, 256:512] = jnp.concatenate([v, e0, rest], axis=0).astype(BF16)
+                field[i, j, :, 512:768] = jnp.concatenate(
+                    [v[1:16], jnp.where(low, e0, none), jnp.where(low, e1, v[0:1]), rest], axis=0
+                ).astype(BF16)
+            return carry
+
+        lax.fori_loop(0, 12, shifts, 0)
 
     def load_chunk(f, n):
         for at, (a, b, cc, d, u), count in runs_of(n):
@@ -375,38 +336,72 @@
 
         lax.fori_loop(0, 10 // NX, one, 0)
 
-    first_conv(0)
-    first_conv(1)
-    turn(1, 1, 1)
-    turn(1, 2, 1)
-    for n in range(2, 5):
-        first_conv(n)
-    for off in (0, 3, 1, 2):
-        end(1, off, 1)
-    for d in range(1, 8):
-        arrived(gall.at[c, lax.rem(q + 8 - d, 8)], gs + d - 1)
-    send(gall.at[c], gall.at[c], gs + 7, sib_dev)
-    for n in range(5, 9):
-        first_conv(n)
-
-    def activate(i, carry):
-        ok = (i + 8 * bx >= 1) & (i + 8 * bx < 65)
-        low = bz == 0
-        hid[i, 5 * by] = jnp.zeros((16, 768), BF16)
-        for j in range(5):
-            h = jnp.where(ok, gelu(acc[i, j]), 0.0)
-            none = jnp.zeros((1, 256), F32)
-            edge = h[16:17]
-            hid[i, y_at + j, :, 0:256] = jnp.concatenate(
-                [jnp.where(low, none, edge), h[0:15]], axis=0
-            ).astype(BF16)
-            hid[i, y_at + j, :, 256:512] = h[0:16].astype(BF16)
-            hid[i, y_at + j, :, 512:768] = jnp.concatenate(
-                [h[1:16], jnp.where(low, edge, none)], axis=0
-            ).astype(BF16)
-        return carry
-
-    lax.fori_loop(0, 10, activate, 0)
+    def activate_hidden():
+        def activate(i, carry):
+            ok = (i + 8 * bx >= 1) & (i + 8 * bx < 65)
+            low = bz == 0
+            hid[i, 5 * by] = jnp.zeros((16, 768), BF16)
+            for j in range(5):
+                h = jnp.where(ok, gelu(acc[i, j]), 0.0)
+                none = jnp.zeros((1, 256), F32)
+                edge = h[16:17]
+                hid[i, y_at + j, :, 0:256] = jnp.concatenate(
+                    [jnp.where(low, none, edge), h[0:15]], axis=0
+                ).astype(BF16)
+                hid[i, y_at + j, :, 256:512] = h[0:16].astype(BF16)
+                hid[i, y_at + j, :, 512:768] = jnp.concatenate(
+                    [h[1:16], jnp.where(low, edge, none)], axis=0
+                ).astype(BF16)
+            return carry
+
+        lax.fori_loop(0, 10, activate, 0)
+
+
+    def run(what, f=0, off=0):
+        if what == "near":
+            wait_near(off)
+            start(0, off, 0)
+            start(1, off, 0)
+        elif what == "far":
+            arrived(blk(off, 0), far + {3: 0, 1: 1, 2: 2}[off])
+            if off != 1:
+                send_near(off)
+                return
+            for n, pos in enumerate((xp, xm, xo)):
+                send(side_block(x), side_block(x), side + n, device(pos, y, z, c))
+        elif what == "side":
+            for n, pos in enumerate((xm, xp, xo)):
+                arrived(side_block(pos), side + n)
+            start(0, 1, 0)
+            start(1, 1, 0)
+        elif what == "turn0":
+            turn(f, off, 0)
+        elif what == "end0":
+            end(f, off, 0)
+            start(f, off, 1)
+        elif what == "turn1":
+            turn(f, off, 1)
+        elif what == "end1":
+            end(f, off, 1)
+        elif what == "conv":
+            first_conv(f)
+        elif what == "sib":
+            from_sib(f)
+        elif what == "edges":
+            edges()
+        elif what == "sums":
+            send_sums()
+        elif what == "shift":
+            shift_field()
+        else:
+            for d in range(1, 8):
+                arrived(gall.at[c, lax.rem(q + 8 - d, 8)], gs + d - 1)
+            send(gall.at[c], gall.at[c], gs + 7, sib_dev)
+
+    send_near(0)
+    for act in PLAN:
+        run(*act)
+    activate_hidden()
 
     from_sib(1)
     for n in range(9):
@@ -427,12 +422,9 @@
         copy.wait_send()
 
 
-def outputs(owned, conv, gall, mom1, mom2, feat, mom1_out, mom2_out):
-    def finish(i, carry):
-        feat[i] = gelu(conv[i]).astype(BF16)
-        return carry
-
-    lax.fori_loop(0, 8, finish, 0)
+def outputs(owned, conv, gall, mom1, mom2, feat, mom1_out, mom2_out, held, sem):
+    copy = pltpu.make_async_copy(conv, held, sem)
+    copy.start()
     for f in range(2):
         here = owned[f] == 1
         for d in range(16):
@@ -445,6 +437,13 @@
                 m, v = mom1[f, at], mom2[f, at]
                 mom1_out[f, at] = jnp.where(here, 0.9 * m + 0.1 * g, m)
                 mom2_out[f, at] = jnp.where(here, 0.95 * v + 0.05 * (g * g), v)
+    copy.wait()
+
+    def finish(i, carry):
+        feat[i] = gelu(held[i]).astype(BF16)
+        return carry
+
+    lax.fori_loop(0, 8, finish, 0)
 
 
 def shards(volumes, grad_parts, master, mom1, mom2, owner):
@@ -491,8 +490,9 @@
     feat, m_out, v_out = pl.pallas_call(
         outputs,
         out_shape=(jax.ShapeDtypeStruct((8, 4, 16, 256), BF16), state, state),
-        in_specs=[smem] + [vmem] * 4,
+        in_specs=[smem, pl.BlockSpec(memory_space=pl.ANY)] + [vmem] * 3,
         out_specs=[vmem] * 3,
+        scratch_shapes=[pltpu.VMEM((8, 4, 16, 256), F32), pltpu.SemaphoreType.DMA],
         compiler_params=pltpu.CompilerParams(vmem_limit_bytes=16 << 20),
     )(owned, conv, gall, *args)
     rows = lax.dynamic_slice_in_dim(pan.reshape(2, 216, 256), 27 * (r // 2), 27, 1)

time: 88.2 us -> 88.7 us (level)
  no operation moved by 1% of the time
where the time goes in v3:
time: 88.7 us; the launch traced here: 88.5 us
  Pallas kernels  84.3 us (95%)
  local copies, waits for them, and re-layouts  2.42 us (3%)
  other arithmetic  1.03 us (1%)
    pallas_call x1, Pallas kernels, shards(): pl.pallas_call(body, out_shape=(jax.ShapeDtypeStruct((8, 4, 16, 256), F32...  82.4 us
    unnamed x11, local copies, waits for them, and re-layouts  2.35 us
    pallas_call x1, Pallas kernels, shards(): pl.pallas_call(outputs, out_shape=(jax.ShapeDtypeStruct((8, 4, 16, 256),...  1.94 us

profile of v3, /device:TPU:1, one launch (start us, length us, event | category | flops | bytes accessed | tf_op | source)
XLA Modules:
  0.0 88.5 jit_solution(12029900623651369051)
XLA Ops:
  0.7 0.0 copy-start.4
  0.7 0.7 copy-done.4
  1.3 0.2 fusion.owned
  1.5 0.0 copy-start
  1.5 0.0 copy-start.1
  1.5 82.4 %shard_map.93 = (f32[8,4,16,256]{3,2,1,0:T(8,128)}, bf16[2,27,8,256]{3,2,1,0:T(8,128)(2,1)}, bf16[2,8,2,2,8,256]{5,4,3,2,1,0:T(8,128)(2,1)}) custom-call(s32[2,32]{1,0:T(2,128)} %owner.1, bf16[8,4,16,256]{3,2,1,0:T(8,128)(2,1)} %bitcast.17, bf16[2,27,8,256]{3,2,1,0:T(8,128)(2,1)} %bitcast.18, f32[2,27,8,256]{3,2,1,0:T(8,128)} %bitcast.16, ...), custom_call_target="tpu_custom_call" | custom-call | tf_op jit(solution)/shard_map/pallas_call | solution.py:458
  83.9 0.0 copy-start.3
  84.0 0.8 dynamic-slice_convert_fusion
  84.9 0.6 copy.13
  85.5 0.0 copy-done
  85.5 0.0 copy-done.1
  85.5 0.0 copy-done.3
  85.5 0.0 copy-start.2
  85.5 1.0 %copy-done.2 = f32[8,4,16,256]{3,2,1,0:T(8,128)S(1)} copy-done((f32[8,4,16,256]{3,2,1,0:T(8,128)S(1)}, f32[8,4,16,256]{3,2,1,0:T(8,128)}, u32[]{:S(2)}) %copy-start.2) | copy-done | bytes 524312
  86.6 1.9 %shard_map.94 = (bf16[8,4,16,256]{3,2,1,0:T(8,128)(2,1)}, f32[2,27,8,256]{3,2,1,0:T(8,128)}, f32[2,27,8,256]{3,2,1,0:T(8,128)}) custom-call(s32[2]{0:T(128)S(1)} %fusion.owned, f32[8,4,16,256]{3,2,1,0:T(8,128)S(1)} %copy-done.2, bf16[2,8,2,2,8,256]{5,4,3,2,1,0:T(8,128)(2,1)S(1)} %copy-done.3, f32[2,27,8,256]{3,2,1,0:T(8,128)S(1)} %bitcast.13, ...), custom_call_target="tpu_custom_call" | custom-call | tf_op jit(solution)/shard_map/pallas_call | solution.py:490
  (2 shorter events, 0.1 us)
Async XLA Ops:
  0.7 0.7 copy-start.4
  1.5 84.0 %copy-start = (f32[1,2,216,256]{3,2,1,0:T(8,128)S(1)}, f32[1,2,216,256]{3,2,1,0:T(8,128)}, u32[]{:S(2)}) copy-start(f32[1,2,216,256]{3,2,1,0:T(8,128)} %param.9) | copy-start | bytes 1327108
  1.5 84.0 %copy-start.1 = (f32[1,2,216,256]{3,2,1,0:T(8,128)S(1)}, f32[1,2,216,256]{3,2,1,0:T(8,128)}, u32[]{:S(2)}) copy-start(f32[1,2,216,256]{3,2,1,0:T(8,128)} %param.10) | copy-start | bytes 1327108
  83.9 1.6 %copy-start.3 = (bf16[2,8,2,2,8,256]{5,4,3,2,1,0:T(8,128)(2,1)S(1)}, bf16[2,8,2,2,8,256]{5,4,3,2,1,0:T(8,128)(2,1)}, u32[]{:S(2)}) copy-start(bf16[2,8,2,2,8,256]{5,4,3,2,1,0:T(8,128)(2,1)} %get-tuple-element.11.gall) | copy-start | bytes 786436
  85.5 1.0 %copy-start.2 = (f32[8,4,16,256]{3,2,1,0:T(8,128)S(1)}, f32[8,4,16,256]{3,2,1,0:T(8,128)}, u32[]{:S(2)}) copy-start(f32[8,4,16,256]{3,2,1,0:T(8,128)} %get-tuple-element.10.conv) | copy-start | bytes 1572868

commit v4 on v3

--- a/solution.py
+++ b/solution.py
@@ -422,11 +422,13 @@
         copy.wait_send()
 
 
-def outputs(owned, conv, gall, mom1, mom2, feat, mom1_out, mom2_out, held, sem):
+def outputs(owner, conv, gall, mom1, mom2, pan, feat, mom1_out, mom2_out, rows, held, panel, sem):
+    s = lax.axis_index("space")
+    r = lax.axis_index("rep")
     copy = pltpu.make_async_copy(conv, held, sem)
     copy.start()
     for f in range(2):
-        here = owned[f] == 1
+        here = owner[f, s] == r
         for d in range(16):
             dc, dl, dx = d // 8, d // 4 % 2, d % 4
             for u in range(2):
@@ -437,6 +439,12 @@
                 m, v = mom1[f, at], mom2[f, at]
                 mom1_out[f, at] = jnp.where(here, 0.9 * m + 0.1 * g, m)
                 mom2_out[f, at] = jnp.where(here, 0.95 * v + 0.05 * (g * g), v)
+    for f in range(2):
+        panel[f, 0:UNITS] = pan[f].astype(F32)
+        panel[f, UNITS] = jnp.zeros((8, 256), F32)
+        at = 27 * (r // 2)
+        near = panel[f, pl.ds(at // 8, 5)].reshape(40, 256)
+        rows[f] = pltpu.roll(near, lax.rem(40 - lax.rem(at, 8), 40), 0)[0:27]
     copy.wait()
 
     def finish(i, carry):
@@ -485,19 +493,26 @@
             collective_id=0, has_side_effects=True, vmem_limit_bytes=56 << 20
         ),
     )(owner, volumes[0, 0], units(grad_parts[0]), units(master), *args)
-    s, r = lax.axis_index("space"), lax.axis_index("rep")
-    owned = (lax.dynamic_slice_in_dim(owner, s, 1, 1)[:, 0] == r).astype(jnp.int32)
-    feat, m_out, v_out = pl.pallas_call(
+    feat, m_out, v_out, rows = pl.pallas_call(
         outputs,
-        out_shape=(jax.ShapeDtypeStruct((8, 4, 16, 256), BF16), state, state),
-        in_specs=[smem, pl.BlockSpec(memory_space=pl.ANY)] + [vmem] * 3,
-        out_specs=[vmem] * 3,
-        scratch_shapes=[pltpu.VMEM((8, 4, 16, 256), F32), pltpu.SemaphoreType.DMA],
-        compiler_params=pltpu.CompilerParams(vmem_limit_bytes=16 << 20),
-    )(owned, conv, gall, *args)
-    rows = lax.dynamic_slice_in_dim(pan.reshape(2, 216, 256), 27 * (r // 2), 27, 1)
-    rows = rows.astype(F32).reshape(2, 2, 3456)
-    share = lax.dynamic_index_in_dim(rows, lax.rem(r, 2), 1, keepdims=False)
+        out_shape=(
+            jax.ShapeDtypeStruct((8, 4, 16, 256), BF16),
+            state,
+            state,
+            jax.ShapeDtypeStruct((2, 27, 256), F32),
+        ),
+        in_specs=[smem, pl.BlockSpec(memory_space=pl.ANY)] + [vmem] * 4,
+        out_specs=[vmem] * 4,
+        scratch_shapes=[
+            pltpu.VMEM((8, 4, 16, 256), F32),
+            pltpu.VMEM((2, UNITS + 1, 8, 256), F32),
+            pltpu.SemaphoreType.DMA,
+        ],
+        compiler_params=pltpu.CompilerParams(vmem_limit_bytes=56 << 20),
+    )(owner, conv, gall, *args, pan)
+    share = lax.dynamic_index_in_dim(
+        rows.reshape(2, 2, 3456), lax.rem(lax.axis_index("rep"), 2), 1, keepdims=False
+    )
     return (
         feat[None, None],
         share,

time: 88.7 us -> 88.3 us (level)
  Pallas kernels: 84.3 us -> 85.8 us
  other arithmetic: 1.03 us -> 0 us
  local copies, waits for them, and re-layouts: 2.42 us -> 1.53 us
    unnamed x11 -> x1, local copies, waits for them, and re-layouts: 2.35 us -> 0.62 us
    pallas_call x1, Pallas kernels: 1.94 us -> 3.57 us  [shards(): pl.pallas_call(outputs, out_shape=(jax.ShapeDtypeStruct((8, 4, 16, 256),...]
where the time goes in v4:
time: 88.3 us; the launch traced here: 88 us
  Pallas kernels  85.8 us (97%)
  local copies, waits for them, and re-layouts  1.53 us (2%)
    pallas_call x1, Pallas kernels, shards(): pl.pallas_call(body, out_shape=(jax.ShapeDtypeStruct((8, 4, 16, 256), F32...  82.3 us
    pallas_call x1, Pallas kernels, shards(): pl.pallas_call(outputs, out_shape=(jax.ShapeDtypeStruct((8, 4, 16, 256),...  3.57 us

profile of v4, /device:TPU:1, one launch (start us, length us, event | category | flops | bytes accessed | tf_op | source)
XLA Modules:
  0.0 88.0 jit_solution(11670410546588607590)
XLA Ops:
  0.6 82.3 %shard_map.93 = (f32[8,4,16,256]{3,2,1,0:T(8,128)}, bf16[2,27,8,256]{3,2,1,0:T(8,128)(2,1)}, bf16[2,8,2,2,8,256]{5,4,3,2,1,0:T(8,128)(2,1)}) custom-call(s32[2,32]{1,0:T(2,128)} %owner.3, bf16[8,4,16,256]{3,2,1,0:T(8,128)(2,1)} %bitcast.16, bf16[2,27,8,256]{3,2,1,0:T(8,128)(2,1)} %bitcast.17, f32[2,27,8,256]{3,2,1,0:T(8,128)} %bitcast.15, ...), custom_call_target="tpu_custom_call" | custom-call | tf_op jit(solution)/shard_map/pallas_call | solution.py:466
  82.9 3.6 %shard_map.94 = (bf16[8,4,16,256]{3,2,1,0:T(8,128)(2,1)}, f32[2,27,8,256]{3,2,1,0:T(8,128)}, f32[2,27,8,256]{3,2,1,0:T(8,128)}, f32[2,27,256]{2,1,0:T(8,128)}) custom-call(s32[2,32]{1,0:T(2,128)} %owner.3, f32[8,4,16,256]{3,2,1,0:T(8,128)} %get-tuple-element.11.conv, bf16[2,8,2,2,8,256]{5,4,3,2,1,0:T(8,128)(2,1)} %get-tuple-element.12.gall, ...), custom_call_target="tpu_custom_call" | custom-call | tf_op jit(solution)/shard_map/pallas_call | solution.py:496
  86.5 0.9 reshape.21
  87.4 0.6 copy.12
  (1 shorter events, 0.0 us)

commit v5 on v4

--- a/solution.py
+++ b/solution.py
@@ -124,16 +124,21 @@
     pair = take(1)
     send(stage.at[1 - c], paired, pair, sib_dev)
     halo = take(N_HALO)
+    inside = {-1: bx > 0, 0: bx >= 0, 1: bx < 7}
+    halo_sent = []
     x_src = {-1: (0, 2), 0: (0, 8), 1: (6, 2)}
     x_dst = {-1: 10, 0: 2, 1: 0}
     for k, (dx, fl, dev) in enumerate(halo_peers):
         sx, nx = x_src[dx]
         sy, dy, ny = (2 * (1 - by), 6 * by, 2) if fl else (0, 2, 4)
-        send(
-            vol.at[pl.ds(sx, nx), pl.ds(sy, ny)],
-            raw.at[pl.ds(x_dst[dx], nx), pl.ds(dy, ny)],
-            halo + k, dev,
+        copy = pltpu.make_async_remote_copy(
+            src_ref=vol.at[pl.ds(sx, nx), pl.ds(sy, ny)],
+            dst_ref=raw.at[pl.ds(x_dst[dx], nx), pl.ds(dy, ny)],
+            send_sem=bar_send.at[halo + k], recv_sem=bar_recv.at[halo + k],
+            device_id=dev, device_id_type=MESH,
         )
+        pl.when(inside[dx])(copy.start)
+        halo_sent.append((inside[dx], copy))
 
     arrived(paired, pair)
     a2a = take(N_A2A)
@@ -268,7 +273,12 @@
             dy, ny = (6 * (1 - by), 2) if fl else (2, 4)
             dst_x = {-1: 0, 0: 2, 1: 10}[dx]
             pairs = raw.at[pl.ds(dst_x, nx), pl.ds(dy, ny)]
-            arrived(pairs, halo + {0: 1, 1: 0, 2: 2, 3: 4, 4: 3}[k])
+            n = halo + {0: 1, 1: 0, 2: 2, 3: 4, 4: 3}[k]
+
+            @pl.when(inside[dx])
+            def _(pairs=pairs, n=n):
+                arrived(pairs, n)
+
 
         def pack(i, carry):
             rows = [raw[i, j].astype(F32) for j in range(8)]
@@ -409,8 +419,15 @@
         load_chunk(1, n)
         lhs = hid[a : a + 8, b : b + 4].reshape(512, 768)
         part = jnp.dot(lhs, wbuf[...].reshape(768, 256), preferred_element_type=F32)
+        rows = acc.at[0:8, 0:4, 0:16]
         part = part.reshape(8, 4, 16, 256)
-        conv[...] = part if n == 0 else conv[...] + part
+        rows[...] = part if n == 0 else rows[...] + part
+
+    def finish(i, carry):
+        conv[i] = gelu(acc[i, 0:4, 0:16]).astype(BF16)
+        return carry
+
+    lax.fori_loop(0, 8, finish, 0)
 
     arrived(gall.at[1 - c], gs + 7)
     sums[...] = gall[...]
@@ -420,12 +437,14 @@
             pan[f, 7 * g : 7 * g + n] = filt[f, yhi, 0, 0, g // 2, g % 2, 0:n]
     for copy in sent:
         copy.wait_send()
-
-
-def outputs(owner, conv, gall, mom1, mom2, pan, feat, mom1_out, mom2_out, rows, held, panel, sem):
+    for there, copy in halo_sent:
+        pl.when(there)(copy.wait_send)
+
+
+def outputs(owner, conv, gall, mom1, mom2, pan, feat, mom1_out, mom2_out, rows, panel, sem):
     s = lax.axis_index("space")
     r = lax.axis_index("rep")
-    copy = pltpu.make_async_copy(conv, held, sem)
+    copy = pltpu.make_async_copy(conv, feat, sem)
     copy.start()
     for f in range(2):
         here = owner[f, s] == r
@@ -447,12 +466,6 @@
         rows[f] = pltpu.roll(near, lax.rem(40 - lax.rem(at, 8), 40), 0)[0:27]
     copy.wait()
 
-    def finish(i, carry):
-        feat[i] = gelu(held[i]).astype(BF16)
-        return carry
-
-    lax.fori_loop(0, 8, finish, 0)
-
 
 def shards(volumes, grad_parts, master, mom1, mom2, owner):
     def units(a):
@@ -466,7 +479,7 @@
     conv, pan, gall = pl.pallas_call(
         body,
         out_shape=(
-            jax.ShapeDtypeStruct((8, 4, 16, 256), F32),
+            jax.ShapeDtypeStruct((8, 4, 16, 256), BF16),
             jax.ShapeDtypeStruct((2, UNITS, 8, 256), BF16),
             jax.ShapeDtypeStruct((2, 8, 2, 2, 8, 256), BF16),
         ),
@@ -502,13 +515,12 @@
             jax.ShapeDtypeStruct((2, 27, 256), F32),
         ),
         in_specs=[smem, pl.BlockSpec(memory_space=pl.ANY)] + [vmem] * 4,
-        out_specs=[vmem] * 4,
+        out_specs=[pl.BlockSpec(memory_space=pl.ANY)] + [vmem] * 3,
         scratch_shapes=[
-            pltpu.VMEM((8, 4, 16, 256), F32),
             pltpu.VMEM((2, UNITS + 1, 8, 256), F32),
             pltpu.SemaphoreType.DMA,
         ],
-        compiler_params=pltpu.CompilerParams(vmem_limit_bytes=56 << 20),
+        compiler_params=pltpu.CompilerParams(vmem_limit_bytes=62 << 20),
     )(owner, conv, gall, *args, pan)
     share = lax.dynamic_index_in_dim(
         rows.reshape(2, 2, 3456), lax.rem(lax.axis_index("rep"), 2), 1, keepdims=False

time: 88.3 us -> 95.9 us (1.086)
  Pallas kernels: 85.8 us -> 93.5 us
    pallas_call x1, Pallas kernels: 3.57 us -> 11.3 us  [shards(): pl.pallas_call(outputs, out_shape=(jax.ShapeDtypeStruct((8, 4, 16, 256),...]
where the time goes in v5:
time: 95.9 us; the launch traced here: 95.7 us
  Pallas kernels  93.5 us (97%)
  local copies, waits for them, and re-layouts  1.53 us (2%)
    pallas_call x1, Pallas kernels, shards(): pl.pallas_call(body, out_shape=(jax.ShapeDtypeStruct((8, 4, 16, 256), BF1...  82.2 us
    pallas_call x1, Pallas kernels, shards(): pl.pallas_call(outputs, out_shape=(jax.ShapeDtypeStruct((8, 4, 16, 256),...  11.3 us

profile of v5, /device:TPU:1, one launch (start us, length us, event | category | flops | bytes accessed | tf_op | source)
XLA Modules:
  0.0 95.7 jit_solution(14262188482080901293)
XLA Ops:
  0.6 82.2 %shard_map.93 = (bf16[8,4,16,256]{3,2,1,0:T(8,128)(2,1)}, bf16[2,27,8,256]{3,2,1,0:T(8,128)(2,1)}, bf16[2,8,2,2,8,256]{5,4,3,2,1,0:T(8,128)(2,1)}) custom-call(s32[2,32]{1,0:T(2,128)} %owner.3, bf16[8,4,16,256]{3,2,1,0:T(8,128)(2,1)} %bitcast.16, bf16[2,27,8,256]{3,2,1,0:T(8,128)(2,1)} %bitcast.17, f32[2,27,8,256]{3,2,1,0:T(8,128)} %bitcast.15, ...), custom_call_target="tpu_custom_call" | custom-call | tf_op jit(solution)/shard_map/pallas_call | solution.py:479
  82.9 11.3 %shard_map.94 = (bf16[8,4,16,256]{3,2,1,0:T(8,128)(2,1)}, f32[2,27,8,256]{3,2,1,0:T(8,128)}, f32[2,27,8,256]{3,2,1,0:T(8,128)}, f32[2,27,256]{2,1,0:T(8,128)}) custom-call(s32[2,32]{1,0:T(2,128)} %owner.3, bf16[8,4,16,256]{3,2,1,0:T(8,128)(2,1)} %get-tuple-element.11.conv, bf16[2,8,2,2,8,256]{5,4,3,2,1,0:T(8,128)(2,1)} %get-tuple-element.12.gall, ...), custom_call_target="tpu_custom_call" | custom-call | tf_op jit(solution)/shard_map/pallas_call | solution.py:509
  94.1 0.9 reshape.21
  95.0 0.6 copy.12
  (1 shorter events, 0.0 us)
